TPU v7x, 32 devices: a whole 2x2x4 slice. The times are simulated.
32 devices in a mesh: blk: 8 (over y, x, core), inner: 4 (over z).
Axes of the slice: x: 2, y: 2, z: 4, core: 2. Of those that a mesh axis runs over, the one named last changes fastest.
Arguments:
- records: float32 [1024, 16, 2048], P('blk', 'inner'), may hold values from -6 to 6
- starts: int32 [16], P('inner'), may hold values from 0 to 1024, as said below
- offsets: int32 [1024, 16], P('blk'), may hold values from -256 to 256, as said below
Outputs:
- correlations: float32 [16, 1024, 768], P('inner', 'blk')
Inputs may be any that keep to these rules, and one draw needn't show every extreme that they name: Segment s uses samples starts[s] to starts[s] + 1023 of its slot. `offsets`: never zero; the partner of channel c is (c + offset) mod 1024.
All inputs are finite; a program needn't handle non-finite values.
Results may differ from a plain program's by a relative error of at most 0.0003.
Values sent between devices are 32-bit elements; how exact they have to be, the bound alone decides.
No kernel may reach another device: no remote copies, remote signals or barrier semaphores. Data moves between devices by JAX's collectives and lax.ppermute only.
A program may use at most 128 MiB of HBM per device.

v0:
```python
import math

import jax
import jax.numpy as jnp
from jax import lax
from jax.sharding import PartitionSpec as P

SEG = 1024
LAGS = 768
HALF = 32
PAIRS = 16
F = 512


def shifted(value, axis, steps):
    count = lax.axis_size(axis)
    pairs = [(source, (source + steps) % count) for source in range(count)]
    return lax.ppermute(value, axis, pairs)


def cut_segment(slot_rows, begin):
    return lax.dynamic_slice_in_dim(slot_rows, begin, SEG, 1)


def lag_rows(bin_ids, half_ids, factor):
    shifts = jnp.arange(LAGS, dtype=jnp.int32) - LAGS // 2
    phase = bin_ids[:, None] * shifts[None, :] % SEG
    angle = 2.0 * jnp.pi / SEG * phase.astype(jnp.float32)
    table = jnp.where(half_ids[:, None] == 0, jnp.cos(angle), -jnp.sin(angle))
    return table * factor


def local(records, starts, offsets):
    channels_here = records.shape[0]
    groups = lax.axis_size("inner")
    group_index = lax.axis_index("inner")
    width = F // groups
    samples = jnp.arange(SEG, dtype=jnp.int32)
    window = 0.5 - 0.5 * jnp.cos(2.0 * jnp.pi * samples.astype(jnp.float32) / SEG)
    pieces = jax.vmap(cut_segment, in_axes=(1, 0), out_axes=1)(records, starts) * window
    segment_rows = pieces.reshape(-1, SEG)
    columns = jnp.arange(2 * F, dtype=jnp.int32)
    column_half = columns // width % 2
    column_bin = columns // (2 * width) * width + columns % width
    phase = samples[:, None] * column_bin[None, :] % SEG
    angle = 2.0 * jnp.pi / SEG * phase.astype(jnp.float32)
    forward = jnp.where(column_half[None, :] == 0, jnp.cos(angle), -jnp.sin(angle))
    spectra = jnp.dot(
        segment_rows, forward, precision=lax.Precision.HIGHEST, preferred_element_type=jnp.float32
    )
    split_spectra = spectra.reshape(-1, groups, 2, width)
    real_part = split_spectra[:, :, 0, :].reshape(-1, F)
    imag_part = split_spectra[:, :, 1, :].reshape(-1, F)
    bins = jnp.arange(F, dtype=jnp.int32)
    distance = jnp.abs(bins[:, None] - bins[None, :])
    distance = jnp.minimum(distance, F - distance)
    band = (distance <= HALF).astype(jnp.float32) / (2 * HALF + 1)
    power = real_part * real_part + imag_part * imag_part
    smooth = jnp.dot(
        power, band, precision=lax.Precision.HIGHEST, preferred_element_type=jnp.float32
    )
    scale = lax.rsqrt(smooth + 1e-06)
    whitened = (split_spectra * scale.reshape(-1, groups, 1, width)).reshape(
        channels_here, -1, 2 * F
    )
    owned = lax.all_to_all(whitened, "inner", split_axis=2, concat_axis=1, tiled=True)
    segment_count = owned.shape[1]
    flat_owned = owned.reshape(channels_here, -1)
    lower_blocks = []
    current = flat_owned
    for hop_number in range(2):
        current = shifted(current, "blk", 1)
        lower_blocks.append(current)
    upper_blocks = []
    current = flat_owned
    for hop_number in range(2):
        current = shifted(current, "blk", -1)
        upper_blocks.append(current)
    extended = jnp.concatenate(
        [lower_blocks[1], lower_blocks[0], flat_owned, upper_blocks[0], upper_blocks[1]], 0
    )
    extended = extended.reshape(5 * channels_here, segment_count, 2, width)
    own_spectra = owned.reshape(channels_here, segment_count, 2, width)
    own_re = own_spectra[:, :, 0, :]
    own_im = own_spectra[:, :, 1, :]
    local_ids = jnp.arange(channels_here, dtype=jnp.int32) + 2 * channels_here
    factor = math.sqrt(segment_count / F)
    local_rows = jnp.arange(2 * width, dtype=jnp.int32)
    local_table = lag_rows(group_index * width + local_rows % width, local_rows // width, factor)

    def one_pair(column_offsets):
        partner = extended[local_ids + column_offsets]
        partner_re = partner[:, :, 0, :]
        partner_im = partner[:, :, 1, :]
        cross_re = jnp.sum(own_re * partner_re + own_im * partner_im, axis=1) / segment_count
        cross_im = jnp.sum(own_im * partner_re - own_re * partner_im, axis=1) / segment_count
        return jnp.concatenate([cross_re, cross_im], 1)

    cross = lax.map(one_pair, offsets.T)
    joined = cross.reshape(lax.axis_size("inner") * (PAIRS // groups) * channels_here, 2 * width)
    result = jnp.dot(
        joined, local_table, precision=lax.Precision.HIGHEST, preferred_element_type=jnp.float32
    )
    return lax.psum_scatter(
        result.reshape(lax.axis_size("inner") * (PAIRS // groups), channels_here, LAGS),
        "inner",
        scatter_dimension=0,
        tiled=True,
    )


def solution(mesh):
    placed = (P("blk", "inner", None), P("inner"), P("blk", None))
    return jax.shard_map(
        local, mesh=mesh, in_specs=placed, out_specs=P("inner", "blk", None), check_vma=False
    )
```

profile of v0, /device:TPU:1, one launch (start us, length us, event | category | flops | bytes accessed | tf_op | source)
XLA Modules:
  0.0 499.1 jit_solution(4393700692033479365)
XLA Ops:
  6.7 6.6 %copy.52 = f32[128,4,2048]{2,0,1:T(8,128)} copy(f32[128,4,2048]{2,1,0:T(4,128)} %param.5) | data formatting | bytes 8388608 | tf_op args[0]
  13.3 12.5 %while.12 = (s32[]{:T(128)}, f32[4,128,2048]{2,1,0:T(8,128)}, s32[4,3]{1,0:T(4,128)S(1)}, f32[4,128,1024]{2,1,0:T(8,128)S(1)}, s32[]{:T(128)}) while((s32[]{:T(128)}, f32[4,128,2048]{2,1,0:T(8,128)}, s32[4,3]{1,0:T(4,128)S(1)}, f32[4,128,1024]{2,1,0:T(8,128)S(1)}, s32[]{:T(128)}) %tuple.60), condition=%wide.while_cond, body=%wide.while_body.sunk | while | flops 2 | bytes 1048693 | solution.py:22
  29.2 25.6 %fusion.7 = f32[512,4,2,128]{0,3,2,1:T(8,128)S(1)} fusion(f32[512,1024,1,1]{1,0,2,3:T(8,128)} %reshape.238, s32[4,2,128]{2,1,0:T(2,128)S(1)} %fusion.58, pred[4,2,128]{2,1,0:T(4,128)(4,1)S(1)} %fusion.60), kind=kOutput, calls=%fused_computation.22 | convolution fusion | flops 6459228160 | bytes 4199424 | tf_op jit(solution)/shard_map/dot_general | solution.py:48
  65.8 52.8 %all_to_all.15 = f32[128,4,1024]{0,1,2:T(4,128)S(1)} all-to-all(f32[128,4,1024]{0,1,2:T(4,128)} %copy.42), channel_id=1, replica_groups=mesh['blk'=8,'inner'=4] {'inner'}, dimensions={2} | all-to-all | bytes 4194304 | tf_op jit(solution)/shard_map/all_to_all | solution.py:66
  121.9 43.7 %collective-permute-done = f32[128,4096]{0,1:T(8,128)} collective-permute-done((f32[128,4096]{0,1:T(8,128)S(1)}, f32[128,4096]{0,1:T(8,128)}, u32[]{:S(2)}, u32[]{:S(2)}) %collective-permute-start) | collective-permute-done | bytes 2097184 | tf_op jit(solution)/shard_map/ppermute | solution.py:18
  175.0 36.1 %collective-permute-done.1 = f32[128,4096]{0,1:T(8,128)} collective-permute-done((f32[128,4096]{0,1:T(8,128)}, f32[128,4096]{0,1:T(8,128)}, u32[]{:S(2)}, u32[]{:S(2)}) %collective-permute-start.1) | collective-permute-done | bytes 2097184 | tf_op jit(solution)/shard_map/ppermute | solution.py:18
  225.7 11.5 %copy.46 = f32[640,16,2,128]{3,1,2,0:T(8,128)} copy(f32[640,16,2,128]{0,3,2,1:T(8,128)} %constant_dynamic-update-slice_fusion) | data formatting | bytes 20971520
  237.2 126.1 %while.13 = (s32[]{:T(128)}, f32[16,128,256]{2,1,0:T(8,128)}, s32[16,128]{1,0:T(8,128)}, f32[640,16,2,128]{3,1,2,0:T(8,128)}, f32[128,16,128]{2,1,0:T(8,128)S(1)}, /*index=5*/f32[128,16,128]{2,1,0:T(8,128)}, s32[]{:T(128)}) while((s32[]{:T(128)}, f32[16,128,256]{2,1,0:T(8,128)}, s32[16,128]{1,0:T(8,128)}, ...), condition=%wide.region_3.4_spmd.clone, body=%wide.region_0.3_spmd.clone.sunk | while | flops 2131586 | bytes 9050705 | solution.py:99
  237.9 4.7 gather_fusion
  245.7 4.7 gather_fusion
  253.6 4.7 gather_fusion
  261.5 4.7 gather_fusion
  269.4 4.7 gather_fusion
  277.3 4.7 gather_fusion
  285.2 4.7 gather_fusion
  293.0 4.7 gather_fusion
  300.9 4.7 gather_fusion
  308.8 4.7 gather_fusion
  316.7 4.7 gather_fusion
  332.5 4.7 gather_fusion
  340.4 4.7 gather_fusion
  348.2 4.7 gather_fusion
  363.3 13.5 %fusion.34 = f32[16,128,768]{2,1,0:T(8,128)} fusion(f32[16,128,256]{2,1,0:T(8,128)} %get-tuple-element.42, s32[768]{0:T(1024)S(1)} %iota_add_fusion, s32[256]{0:T(256)S(1)} %fusion.63, pred[256]{0:T(512)(128)(4,1)S(1)} %fusion.64), kind=kOutput, calls=%fused_computation.59 | convolution fusion | flops 4835180544 | bytes 8392960 | tf_op jit(solution)/shard_map/dot_general | solution.py:101
  376.8 115.4 %reduce-scatter.2.cloned.1.call-done = f32[4,128,768]{2,1,0:T(8,128)} async-done(((f32[16,128,768]{2,1,0:T(8,128)}), f32[4,128,768]{2,1,0:T(8,128)}) %reduce-scatter.2.cloned.1.call-update) | async-done | bytes 1572880 | tf_op jit(solution)/shard_map/reduce_scatter | solution.py:104
  (135 shorter events, 114.8 us)
Async XLA Ops:
  6.5 485.7 %reduce-scatter.2.cloned.1.call-start = ((), (), s32[]{:S(2)}) async-start(), calls=%async_computation.2 | async-start | bytes 7864320 | tf_op jit(solution)/shard_map/reduce_scatter | solution.py:104
  6.6 6.6 %copy-start = (s32[4]{0:T(128)S(1)}, s32[4]{0:T(128)}, u32[]{:S(2)}) copy-start(s32[4]{0:T(128)} %param.6) | copy-start | bytes 52
  118.9 46.6 %collective-permute-start = (f32[128,4096]{0,1:T(8,128)S(1)}, f32[128,4096]{0,1:T(8,128)}, u32[]{:S(2)}, u32[]{:S(2)}) collective-permute-start(f32[128,4096]{0,1:T(8,128)S(1)} %bitcast.78), channel_id=1, source_target_pairs={{0,4},{4,8},{8,12},{12,16},{16,20},{20,24},{24,28},{28,0},{1,5},{5... | collective-permute-start | bytes 6291464 | tf_op jit(solution)/shard_map/ppermute | solution.py:18
  121.9 47.2 %collective-permute-start.2 = (f32[128,4096]{0,1:T(8,128)S(1)}, f32[128,4096]{0,1:T(8,128)}, u32[]{:S(2)}, u32[]{:S(2)}) collective-permute-start(f32[128,4096]{0,1:T(8,128)S(1)} %bitcast.79), channel_id=1, source_target_pairs={{0,28},{4,0},{8,4},{12,8},{16,12},{20,16},{24,20},{28,24},{1,29},{... | collective-permute-start | bytes 6291464 | tf_op jit(solution)/shard_map/ppermute | solution.py:18
  165.5 45.6 %collective-permute-start.1 = (f32[128,4096]{0,1:T(8,128)}, f32[128,4096]{0,1:T(8,128)}, u32[]{:S(2)}, u32[]{:S(2)}) collective-permute-start(f32[128,4096]{0,1:T(8,128)} %collective-permute-done), channel_id=1, source_target_pairs={{0,4},{4,8},{8,12},{12,16},{16,20},{20,24},{24,28},{28,0},{1,5},{5... | collective-permute-start | bytes 6291464 | tf_op jit(solution)/shard_map/ppermute | solution.py:18
  169.1 53.3 %collective-permute-start.3 = (f32[128,4096]{0,1:T(8,128)}, f32[128,4096]{0,1:T(8,128)}, u32[]{:S(2)}, u32[]{:S(2)}) collective-permute-start(f32[128,4096]{0,1:T(8,128)} %collective-permute-done.2), channel_id=1, source_target_pairs={{0,28},{4,0},{8,4},{12,8},{16,12},{20,16},{24,20},{28,24},{1,29},{... | collective-permute-start | bytes 6291464 | tf_op jit(solution)/shard_map/ppermute | solution.py:18
Sparse Core Ops, SparseCore 0:
  376.9 115.2 reduce-scatter.1
where the time goes:
time: 502 us; the launch traced here: 499 us
  waiting for transfers between devices  196 us (39%)
  local copies, waits for them, and re-layouts  137 us (27%)
  blocking collectives  52.8 us (11%)
  other arithmetic  52.2 us (10%)
  matrix products  41.2 us (8%)
  between operations  13.5 us (3%)
  starting transfers between devices  5.56 us (1%)
    reduce_scatter x1, waiting for transfers between devices, local(): lax.psum_scatter(result.reshape(lax.axis_size('inner') * (PAIRS // groups...  115 us
    ppermute x4, waiting for transfers between devices, shifted(): return lax.ppermute(value, axis, pairs)  80.7 us
    gather x16, local copies, waits for them, and re-layouts, one_pair(): partner = extended[local_ids + column_offsets]  74.5 us
    all_to_all x1, blocking collectives, local(): lax.all_to_all(whitened, 'inner', split_axis=2, concat_axis=1, tiled=True)  52.8 us
    unnamed x12, local copies, waits for them, and re-layouts  33.7 us
    reduce_sum x16, other arithmetic, one_pair(): jnp.sum(own_re * partner_re + own_im * partner_im, axis=1) / segment_count  29.2 us
    dot_general x1, matrix products, local(): jnp.dot(segment_rows, forward, precision=lax.Precision.HIGHEST, preferred...  25.6 us
    dot_general x1, matrix products, local(): jnp.dot(joined, local_table, precision=lax.Precision.HIGHEST, preferred_e...  13.5 us
  transfers between devices with their start and end apart: 5, of which 4 were waited for; matrix products, arithmetic and copies ran while one was open for 3% of the time, Pallas kernels for 0%

commit v1 on v0

v1 whole, which is shorter than its diff:
```python
import functools
import math

import jax
import jax.numpy as jnp
import numpy as np
from jax import lax
from jax.experimental import pallas as pl
from jax.experimental.pallas import tpu as pltpu
from jax.sharding import PartitionSpec as P

SEG = 1024
LAGS = 768
HALF = 32
F = 512
LANES = 128
EPS = 1e-06


def bin_order():
    m = np.arange(128)
    return np.concatenate([4 * m, 4 * m + 2, 4 * m + 1, 4 * m[::-1] + 3])


def transform_tables():
    u = np.arange(256)

    def angle(bins):
        return 2 * np.pi / SEG * (bins[:, None] * u[None, :] % SEG)

    m = np.arange(128)
    even = [angle(4 * m), angle(4 * m + 2)]
    even = [np.concatenate([np.cos(a), -np.sin(a)], 0) for a in even]
    a = angle(4 * np.arange(256) + 1)
    sign = np.where(np.arange(256) < 128, 1.0, -1.0)[:, None]
    odd_re = np.concatenate([np.cos(a), -np.sin(a)], 1)
    odd_im = np.concatenate([-np.sin(a), -np.cos(a)], 1) * sign
    odd = np.concatenate([odd_re, odd_im], 0)
    return [t.astype(np.float32) for t in (even[0], even[1], odd)]


def band_table():
    order = bin_order()
    distance = np.abs(order[:, None] - order[None, :])
    distance = np.minimum(distance, F - distance)
    return (distance <= HALF).astype(np.float32)


def lag_table(width, segment_count):
    shifts = np.arange(LAGS) - LAGS // 2
    angle = 2 * np.pi / SEG * (bin_order()[:, None] * shifts[None, :] % SEG)
    table = np.stack([np.cos(angle), -np.sin(angle)], 0).reshape(2, F // width, width, LAGS)
    factor = math.sqrt(segment_count / F) / segment_count
    return (table.transpose(1, 0, 2, 3).reshape(2 * F, LAGS) * factor).astype(np.float32)


def halves(x):
    high = x.astype(jnp.bfloat16)
    return high, (x - high.astype(jnp.float32)).astype(jnp.bfloat16)


def dot_nt(a, b, precision=None):
    return lax.dot_general(
        a, b, (((1,), (1,)), ((), ())), precision=precision, preferred_element_type=jnp.float32
    )


def dot_tn(a, b):
    return lax.dot_general(a, b, (((0,), (0,)), ((), ())), preferred_element_type=jnp.float32)


def whiten_kernel(records_ref, window_ref, even0_ref, even2_ref, odd_ref, band_ref, out_ref):
    count = records_ref.shape[1]
    rows = out_ref.shape[3]
    sums, alternating, odds = [], [], []
    for s in range(count):
        folded = records_ref[:, s, :SEG] * window_ref[s : s + 1, :SEG]
        folded += records_ref[:, s, SEG:] * window_ref[s : s + 1, SEG:]
        x = [folded[:, 256 * j : 256 * (j + 1)] for j in range(4)]
        sums.append((x[0] + x[2]) + (x[1] + x[3]))
        alternating.append((x[0] + x[2]) - (x[1] + x[3]))
        odds.append(jnp.concatenate([x[0] - x[2], x[1] - x[3]], 1))
    highest = lax.Precision.HIGHEST
    s0 = dot_nt(even0_ref[...], jnp.concatenate(sums, 0), highest)
    s2 = dot_nt(even2_ref[...], jnp.concatenate(alternating, 0), highest)
    s1 = dot_nt(odd_ref[...], jnp.concatenate(odds, 0), highest)
    re = jnp.concatenate([s0[:128], s2[:128], s1[:256]], 0)
    im = jnp.concatenate([s0[128:], s2[128:], s1[256:]], 0)
    high, low = halves(re * re + im * im)
    band = band_ref[...]
    smooth = jnp.dot(band, high, preferred_element_type=jnp.float32)
    smooth += jnp.dot(band, low, preferred_element_type=jnp.float32)
    scale = lax.rsqrt(smooth * (1.0 / (2 * HALF + 1)) + EPS)
    re, im = re * scale, im * scale
    for s in range(count):
        lanes = slice(s * LANES, (s + 1) * LANES)
        out_ref[:, s, 0] = re[:, lanes].reshape(-1, rows, LANES)
        out_ref[:, s, 1] = im[:, lanes].reshape(-1, rows, LANES)


def whiten(records, starts, rows):
    count = records.shape[1]
    samples = jnp.arange(SEG, dtype=jnp.int32)[None, :]
    begin = starts[:, None].astype(jnp.int32)
    phase = (samples - begin) % SEG
    window = 0.5 - 0.5 * jnp.cos(2.0 * jnp.pi / SEG * phase.astype(jnp.float32))
    early = samples >= begin
    window = jnp.concatenate([jnp.where(early, window, 0.0), jnp.where(early, 0.0, window)], 1)
    tables = [jnp.asarray(t) for t in transform_tables()]
    band = jnp.asarray(band_table(), jnp.bfloat16)
    return pl.pallas_call(
        whiten_kernel,
        out_shape=jax.ShapeDtypeStruct((F // rows, count, 2, rows, LANES), jnp.float32),
        compiler_params=pltpu.CompilerParams(vmem_limit_bytes=56 << 20),
    )(records, window, *tables, band)


def pair_kernel(index_ref, spectra_ref, sum_ref, out_ref, wide_ref, product_ref, *, width):
    block = pl.program_id(0)
    blocks, depth = spectra_ref.shape[:2]
    pairs = index_ref.shape[1]
    groups = out_ref.shape[1]
    share = pairs // groups

    @pl.when(block == 0)
    def _():
        if depth < 4:
            wide_ref[...] = jnp.zeros(wide_ref.shape, wide_ref.dtype)

        def build(i, carry):
            for r in range(depth):
                turned = spectra_ref[i, r].T
                for h in range(2):
                    wide_ref[pl.ds(i * 8 * LANES + 2 * r + h, LANES, stride=8), :] = turned
            return carry

        lax.fori_loop(0, blocks, build, 0)

    row = lax.broadcasted_iota(jnp.int32, (8, LANES), 0)
    lane = lax.broadcasted_iota(jnp.int32, (8, LANES), 1)
    bit0, bit1, bit2 = row % 2 == 0, row // 2 % 2 == 0, row // 4 == 0
    is_re = lane // width % 2 == 0

    def roll(x, steps):
        return pltpu.roll(x, steps % 8, 0)

    def fold4(a, b):
        return jnp.where(bit2, a, b) + roll(jnp.where(bit2, b, a), 4)

    def fold2(a, b):
        return jnp.where(bit1, a + roll(a, -2), b + roll(b, 2))

    def group(g, carry):
        first = pl.multiple_of(g * 8, 8)
        own = []
        for j in range(8):
            at = pl.multiple_of((block * LANES + first + j) * 8, 8)
            w = wide_ref[pl.ds(at, 8), :]
            turned = jnp.where(is_re, pltpu.roll(w, LANES - width, 1), -pltpu.roll(w, width, 1))
            own.append(jnp.where(bit0, w, turned))
        for k in range(pairs):
            p = []
            for j in range(8):
                at = pl.multiple_of(index_ref[0, k, first + j], 8)
                p.append(own[j] * wide_ref[pl.ds(at, 8), :])
            even = fold2(fold4(p[0], p[4]), fold4(p[2], p[6]))
            odd = fold2(fold4(p[1], p[5]), fold4(p[3], p[7]))
            product_ref[0, k, pl.ds(first, 8), :] = jnp.where(bit0, even, roll(odd, 1))
            product_ref[1, k, pl.ds(first, 8), :] = jnp.where(bit0, roll(even, -1), odd)
        return carry

    lax.fori_loop(0, LANES // 8, group, 0)
    for z in range(groups):
        for h in range(2):
            x = product_ref[h, z * share : (z + 1) * share].reshape(share * LANES, LANES)
            out_ref[0, z, h] = dot_nt(sum_ref[...], jnp.concatenate(halves(x), 1))


def pair_products(spectra, index, groups, width):
    blocks = spectra.shape[0]
    pairs = index.shape[1]
    rows = max(width, 8)
    summing = np.zeros((rows, LANES), np.float32)
    summing[np.arange(LANES) % width, np.arange(LANES)] = 1
    summing = jnp.asarray(np.concatenate([summing, summing], 1), jnp.bfloat16)
    shape = (groups, 2, rows, pairs // groups * LANES)
    return pl.pallas_call(
        functools.partial(pair_kernel, width=width),
        grid=(blocks,),
        in_specs=[
            pl.BlockSpec((1, pairs, LANES), lambda b: (b, 0, 0), memory_space=pltpu.SMEM),
            pl.BlockSpec(spectra.shape, lambda b: (0,) * 4),
            pl.BlockSpec(summing.shape, lambda b: (0, 0)),
        ],
        out_specs=pl.BlockSpec((1, *shape), lambda b: (b, 0, 0, 0, 0)),
        out_shape=jax.ShapeDtypeStruct((blocks, *shape), jnp.float32),
        scratch_shapes=[
            pltpu.VMEM((blocks * LANES * 8, LANES), jnp.float32),
            pltpu.VMEM((2, pairs, LANES, LANES), jnp.float32),
        ],
        compiler_params=pltpu.CompilerParams(vmem_limit_bytes=56 << 20),
    )(index, spectra, summing)


def lag_kernel(cross_ref, high_ref, low_ref, out_ref):
    high, low = halves(cross_ref[...])
    total = dot_tn(high, low_ref[...]) + dot_tn(low, high_ref[...])
    out_ref[0] = total + dot_tn(high, high_ref[...])


def lag_transform(cross, table):
    count = cross.shape[1] // LANES
    high = table.astype(jnp.bfloat16)
    low = (table - high.astype(np.float32)).astype(jnp.bfloat16)
    return pl.pallas_call(
        lag_kernel,
        grid=(count,),
        in_specs=[
            pl.BlockSpec((2 * F, LANES), lambda i: (0, i)),
            pl.BlockSpec((2 * F, LAGS), lambda i: (0, 0)),
            pl.BlockSpec((2 * F, LAGS), lambda i: (0, 0)),
        ],
        out_specs=pl.BlockSpec((1, LANES, LAGS), lambda i: (i, 0, 0)),
        out_shape=jax.ShapeDtypeStruct((count, LANES, LAGS), jnp.float32),
        compiler_params=pltpu.CompilerParams(vmem_limit_bytes=56 << 20),
    )(cross, jnp.asarray(high), jnp.asarray(low))


def local(records, starts, offsets):
    axes = ("blk", "inner")
    blocks, groups = lax.axis_size("blk"), lax.axis_size("inner")
    devices = blocks * groups
    width = F // devices
    here, count = records.shape[:2]
    channels = here * blocks
    ids = jnp.arange(here, dtype=jnp.int32)[:, None] + lax.axis_index("blk") * here
    index = (((ids + offsets) % channels) * 8).T
    index = lax.all_gather(index, "blk", axis=0)
    rows = max(width, 8)
    white = whiten(records, starts, rows)
    split = rows // width
    white = white.reshape(-1, count, 2, split, width, LANES).transpose(0, 3, 1, 2, 4, 5)
    white = white.reshape(devices, count * 2 * width, LANES)
    spectra = lax.all_to_all(white, axes, 0, 0, tiled=True)
    spectra = spectra.reshape(blocks, -1, LANES, LANES)
    cross = pair_products(spectra, index, groups, width)
    cross = cross[:, :, :, :width].reshape(devices, 2 * width, -1)
    cross = lax.all_to_all(cross, axes, 0, 0, tiled=True)
    return lag_transform(cross.reshape(2 * F, -1), lag_table(width, count * groups))


def solution(mesh):
    placed = (P("blk", "inner", None), P("inner"), P("blk", None))
    return jax.shard_map(
        local, mesh=mesh, in_specs=placed, out_specs=P("inner", "blk", None), check_vma=False
    )
```

time: 502 us -> 160 us (0.32)
  waiting for transfers between devices: 196 us -> 28.2 us
  local copies, waits for them, and re-layouts: 137 us -> 1.31 us
  other arithmetic: 52.2 us -> 1.51 us
  Pallas kernels: 0 us -> 48.9 us
  matrix products: 41.2 us -> 0 us
  blocking collectives: 52.8 us -> 72.4 us
  between operations: 13.5 us -> 0.04 us
    reduce_scatter x1 -> x0, waiting for transfers between devices: 115 us -> none  [local(): lax.psum_scatter(result.reshape(lax.axis_size('inner') * (PAIRS // groups...]
    gather x28 -> x0, local copies, waits for them, and re-layouts: 86.9 us -> none  [the longest x16 74.5 us: one_pair(): partner = extended[local_ids + column_offsets]]
    ppermute x4 -> x0, waiting for transfers between devices: 80.7 us -> none  [shifted(): return lax.ppermute(value, axis, pairs)]
    pallas_call x0 -> x3, Pallas kernels: none -> 48.9 us  [the longest x1 33.9 us: pair_products(): pl.pallas_call(functools.partial(pair_kernel, width=width), grid=(blocks,...]
    dot_general x3 -> x0, matrix products: 41.2 us -> none  [the longest x1 25.6 us: local(): jnp.dot(segment_rows, forward, precision=lax.Precision.HIGHEST, preferred...]
    unnamed x12 -> x4, local copies, waits for them, and re-layouts: 33.7 us -> 1.31 us
    reduce_sum x16 -> x0, other arithmetic: 29.2 us -> none  [one_pair(): jnp.sum(own_re * partner_re + own_im * partner_im, axis=1) / segment_count]
    all_to_all x0 -> x1, waiting for transfers between devices: none -> 28.2 us  [local(): spectra = lax.all_to_all(white, axes, 0, 0, tiled=True)]
  transfers between devices with their start and end apart: 5 -> 1, of which waited for: 4 -> 1; matrix products, arithmetic and copies ran while one was open for 3% -> 0% of each run, Pallas kernels for 0% -> 0%
where the time goes in v1:
time: 160 us; the launch traced here: 159 us
  blocking collectives  72.4 us (45%)
  Pallas kernels  48.9 us (31%)
  waiting for transfers between devices  28.2 us (18%)
  starting transfers between devices  7.1 us (4%)
    all_to_all x1, blocking collectives, local(): cross = lax.all_to_all(cross, axes, 0, 0, tiled=True)  52.3 us
    pallas_call x1, Pallas kernels, pair_products(): pl.pallas_call(functools.partial(pair_kernel, width=width), grid=(blocks,...  33.9 us
    all_to_all x1, waiting for transfers between devices, local(): spectra = lax.all_to_all(white, axes, 0, 0, tiled=True)  28.2 us
    all_gather x1, blocking collectives, local(): index = lax.all_gather(index, 'blk', axis=0)  20 us
    pallas_call x1, Pallas kernels, whiten(): pl.pallas_call(whiten_kernel, out_shape=jax.ShapeDtypeStruct((F // rows,...  8.5 us
    all_to_all x1, starting transfers between devices, local(): spectra = lax.all_to_all(white, axes, 0, 0, tiled=True)  7.1 us
    pallas_call x1, Pallas kernels, lag_transform(): pl.pallas_call(lag_kernel, grid=(count,), in_specs=[pl.BlockSpec((2 * F,...  6.51 us
  transfers between devices with their start and end apart: 1, of which 1 were waited for; matrix products, arithmetic and copies ran while one was open for 0% of the time, Pallas kernels for 0%

profile of v1, /device:TPU:1, one launch (start us, length us, event | category | flops | bytes accessed | tf_op | source)
XLA Modules:
  0.0 159.4 jit_solution(14132957623746732200)
XLA Ops:
  0.0 0.9 fusion.7
  0.9 0.6 pad_maximum_fusion.window_ref
  1.5 8.5 %shard_map.100 = f32[32,4,2,16,128]{4,3,2,1,0:T(8,128)} custom-call(f32[128,4,2048]{2,1,0:T(4,128)} %records_ref.1, f32[4,2048]{1,0:T(4,128)} %pad_maximum_fusion.window_ref, f32[256,256]{1,0:T(8,128)} %constant.53.clone.even0_ref, f32[256,256]{1,0:T(8,128)} %constant.54.clone.even2_ref, f32[512,512]{1,0:T(8,128)} %constant.55.clone.odd_ref, ...), custom_call_target="tpu_custom_call" | custom-call | tf_op jit(solution)/shard_map/pallas_call | solution.py:111
  10.0 0.0 copy-start.1
  10.0 7.1 %all-to-all-start = ((f32[32,128,128]{2,1,0:T(8,128)}), f32[32,128,128]{2,1,0:T(8,128)S(1)}, u32[]{:S(2)}, u32[]{:S(2)}) async-start(f32[32,128,128]{2,1,0:T(8,128)} %bitcast.10), calls=%async_computation | async-start | bytes 4194304 | tf_op jit(solution)/shard_map/all_to_all | solution.py:244
  17.1 0.0 copy-done.1
  17.2 20.0 %all-gather = s32[128,128]{1,0:T(8,128)} all-gather(s32[16,128]{1,0:T(8,128)S(1)} %fusion.10), channel_id=2, replica_groups=mesh['blk'=8,'inner'=4] {'blk'}, dimensions={0}, use_global_device_ids=true | all-gather | bytes 73728 | tf_op jit(solution)/shard_map/all_gather | solution.py:238
  37.2 28.2 %all-to-all-done = f32[32,128,128]{2,1,0:T(8,128)S(1)} async-done(((f32[32,128,128]{2,1,0:T(8,128)}), f32[32,128,128]{2,1,0:T(8,128)S(1)}, u32[]{:S(2)}, u32[]{:S(2)}) %all-to-all-start) | async-done | bytes 2097184 | tf_op jit(solution)/shard_map/all_to_all | solution.py:244
  65.4 0.0 copy-start
  65.4 1.3 copy-done
  66.7 33.9 %shard_map.101 = f32[8,4,2,16,512]{4,3,2,1,0:T(8,128)} custom-call(s32[8,16,128]{2,1,0:T(8,128)} %bitcast.11, f32[8,4,128,128]{3,2,1,0:T(8,128)} %bitcast.7, bf16[16,256]{1,0:T(8,128)(2,1)} %constant.57.clone.sum_ref), custom_call_target="tpu_custom_call" | custom-call | tf_op jit(solution)/shard_map/pallas_call | solution.py:187
  100.6 52.3 %all_to_all.10 = f32[32,32,512]{2,1,0:T(8,128)} all-to-all(f32[32,32,512]{2,1,0:T(8,128)} %bitcast.8), channel_id=1, replica_groups=mesh['blk'=8,'inner'=4] {'blk','inner'}, dimensions={0} | all-to-all | bytes 4194304 | tf_op jit(solution)/shard_map/all_to_all | solution.py:248
  152.9 6.5 %shard_map.102 = f32[4,128,768]{2,1,0:T(8,128)} custom-call(f32[1024,512]{1,0:T(8,128)} %bitcast.9, bf16[1024,768]{1,0:T(8,128)(2,1)} %constant.58.clone.high_ref, bf16[1024,768]{1,0:T(8,128)(2,1)} %constant.59.clone.low_ref), custom_call_target="tpu_custom_call" | custom-call | tf_op jit(solution)/shard_map/pallas_call | solution.py:215
  (2 shorter events, 0.0 us)
Async XLA Ops:
  10.0 7.1 %copy-start.1 = (s32[128,16]{0,1:T(8,128)S(1)}, s32[128,16]{0,1:T(8,128)}, u32[]{:S(2)}) copy-start(s32[128,16]{0,1:T(8,128)} %param.12) | copy-start | bytes 24580
  10.0 55.4 %all-to-all-start = ((f32[32,128,128]{2,1,0:T(8,128)}), f32[32,128,128]{2,1,0:T(8,128)S(1)}, u32[]{:S(2)}, u32[]{:S(2)}) async-start(f32[32,128,128]{2,1,0:T(8,128)} %bitcast.10), calls=%async_computation | async-start | bytes 4194304 | tf_op jit(solution)/shard_map/all_to_all | solution.py:244
  65.4 1.3 copy-start

commit v2 on v1

v2 whole, which is shorter than its diff:
```python
import functools
import math

import jax
import jax.numpy as jnp
import numpy as np
from jax import lax
from jax.experimental import pallas as pl
from jax.experimental.pallas import tpu as pltpu
from jax.sharding import PartitionSpec as P

SEG = 1024
LAGS = 768
HALF = 32
REACH = 256
F = 512
LANES = 128
EPS = 1e-06


def bin_order():
    m = np.arange(128)
    return np.concatenate([4 * m, 4 * m + 2, 4 * m + 1, 4 * m[::-1] + 3])


def transform_tables():
    u = np.arange(256)

    def angle(bins):
        return 2 * np.pi / SEG * (bins[:, None] * u[None, :] % SEG)

    m = np.arange(128)
    even = [angle(4 * m), angle(4 * m + 2)]
    even = [np.concatenate([np.cos(a), -np.sin(a)], 0) for a in even]
    a = angle(4 * np.arange(256) + 1)
    sign = np.where(np.arange(256) < 128, 1.0, -1.0)[:, None]
    odd_re = np.concatenate([np.cos(a), -np.sin(a)], 1)
    odd_im = np.concatenate([-np.sin(a), -np.cos(a)], 1) * sign
    odd = np.concatenate([odd_re, odd_im], 0)
    return [t.astype(np.float32) for t in (even[0], even[1], odd)]


def band_table():
    order = bin_order()
    distance = np.abs(order[:, None] - order[None, :])
    distance = np.minimum(distance, F - distance)
    return (distance <= HALF).astype(np.float32)


def lag_table(width, segment_count):
    shifts = np.arange(LAGS) - LAGS // 2
    angle = 2 * np.pi / SEG * (bin_order()[:, None] * shifts[None, :] % SEG)
    table = np.stack([np.cos(angle), -np.sin(angle)], 0).reshape(2, F // width, width, LAGS)
    factor = math.sqrt(segment_count / F) / segment_count
    return (table.transpose(1, 0, 2, 3).reshape(2 * F, LAGS) * factor).astype(np.float32)


def halves(x):
    high = x.astype(jnp.bfloat16)
    return high, (x - high.astype(jnp.float32)).astype(jnp.bfloat16)


def dot_nt(a, b, precision=None):
    return lax.dot_general(
        a, b, (((1,), (1,)), ((), ())), precision=precision, preferred_element_type=jnp.float32
    )


def dot_tn(a, b):
    return lax.dot_general(a, b, (((0,), (0,)), ((), ())), preferred_element_type=jnp.float32)


def hann_table():
    window = 0.5 - 0.5 * np.cos(2 * np.pi / SEG * np.arange(SEG))
    return np.tile(window[None, :], (8, 1)).astype(np.float32)


def whiten_kernel(
    starts_ref, records_ref, hann_ref, even0_ref, even2_ref, odd_ref, band_ref, out_ref, folded_ref
):
    step = pl.program_id(0)
    part, count = records_ref.shape[:2]
    rows = out_ref.shape[3]
    place = pl.multiple_of(step * part, part)
    samples = lax.broadcasted_iota(jnp.int32, (8, SEG), 1)
    for s in range(count):
        begin = starts_ref[s]
        window = pltpu.roll(hann_ref[...], lax.rem(begin, SEG), 1)[:1]
        early = jnp.where(samples >= begin, 1.0, 0.0)[:1] * window
        late = window - early
        x = records_ref[:, s, :SEG] * early + records_ref[:, s, SEG:] * late
        x = [x[:, 256 * j : 256 * (j + 1)] for j in range(4)]
        at = pl.ds(s * LANES + place, part)
        folded_ref[at, :256] = (x[0] + x[2]) + (x[1] + x[3])
        folded_ref[at, 256:512] = (x[0] + x[2]) - (x[1] + x[3])
        folded_ref[at, 512:768] = x[0] - x[2]
        folded_ref[at, 768:] = x[1] - x[3]

    @pl.when(step == pl.num_programs(0) - 1)
    def _():
        highest = lax.Precision.HIGHEST
        s0 = dot_nt(even0_ref[...], folded_ref[:, :256], highest)
        s2 = dot_nt(even2_ref[...], folded_ref[:, 256:512], highest)
        s1 = dot_nt(odd_ref[...], folded_ref[:, 512:], highest)
        re = jnp.concatenate([s0[:128], s2[:128], s1[:256]], 0)
        im = jnp.concatenate([s0[128:], s2[128:], s1[256:]], 0)
        high, low = halves(re * re + im * im)
        band = band_ref[...]
        smooth = jnp.dot(band, high, preferred_element_type=jnp.float32)
        smooth += jnp.dot(band, low, preferred_element_type=jnp.float32)
        scale = lax.rsqrt(smooth * (1.0 / (2 * HALF + 1)) + EPS)
        re, im = re * scale, im * scale
        for s in range(count):
            lanes = slice(s * LANES, (s + 1) * LANES)
            out_ref[:, s, 0] = re[:, lanes].reshape(-1, rows, LANES)
            out_ref[:, s, 1] = im[:, lanes].reshape(-1, rows, LANES)


def whiten(records, starts, rows):
    here, count, slot = records.shape
    part = 32
    tables = [jnp.asarray(t) for t in (hann_table(), *transform_tables())]
    tables.append(jnp.asarray(band_table(), jnp.bfloat16))
    shape = (F // rows, count, 2, rows, LANES)
    return pl.pallas_call(
        whiten_kernel,
        grid=(here // part,),
        in_specs=[
            pl.BlockSpec(memory_space=pltpu.SMEM),
            pl.BlockSpec((part, count, slot), lambda i: (i, 0, 0)),
            *[pl.BlockSpec(memory_space=pltpu.VMEM) for _ in tables],
        ],
        out_specs=pl.BlockSpec(shape, lambda i: (0,) * 5),
        out_shape=jax.ShapeDtypeStruct(shape, jnp.float32),
        scratch_shapes=[pltpu.VMEM((count * LANES, SEG), jnp.float32)],
        compiler_params=pltpu.CompilerParams(vmem_limit_bytes=32 << 20),
    )(starts, records, *tables)


def pair_kernel(index_ref, spectra_ref, out_ref, wide_ref, hot_ref, *, reach, turned):
    block = pl.program_id(0)
    blocks, terms, _, rows, _ = spectra_ref.shape
    pairs = index_ref.shape[1]
    groups = out_ref.shape[1]
    share = pairs // groups
    span = 2 * reach + 1

    @pl.when(block == 0)
    def _():
        def build(i, carry):
            wide_ref[i, 0], wide_ref[i, 1] = halves(spectra_ref[i].reshape(-1, LANES))
            return carry

        lax.fori_loop(0, blocks, build, 0)

    near = [lax.rem(block + (blocks - reach + j), blocks) for j in range(span)]
    left = jnp.concatenate([wide_ref[i, h] for i in near for h in range(2)], 1)
    ids = lax.broadcasted_iota(jnp.int32, (LANES, LANES), 0)

    def put(k, h, rows_here, x):
        z, q = k // share, k % share
        out_ref[0, z, h, rows_here, q * LANES : (q + 1) * LANES] = x

    def by_product(n, ks):
        for i, k in enumerate(ks):
            row = index_ref[0, k : k + 1, :]
            for j in range(span):
                hot = jnp.where(ids + j * LANES == row, 1.0, 0.0).astype(jnp.bfloat16)
                for h in range(2):
                    at = (2 * j + h) * LANES
                    hot_ref[n % 2, at : at + LANES, i * LANES : (i + 1) * LANES] = hot
        found = jnp.dot(
            left, hot_ref[n % 2, :, : len(ks) * LANES], preferred_element_type=jnp.float32
        )
        found = found.reshape(terms, 2, rows, -1)
        for i, k in enumerate(ks):
            lanes = slice(i * LANES, (i + 1) * LANES)
            re = im = 0
            for t in range(terms):
                partner_re, partner_im = found[t, 0, :, lanes], found[t, 1, :, lanes]
                own_re, own_im = spectra_ref[block, t, 0], spectra_ref[block, t, 1]
                re = re + (own_re * partner_re + own_im * partner_im)
                im = im + (own_im * partner_re - own_re * partner_im)
            put(k, 0, slice(0, rows), re)
            put(k, 1, slice(0, rows), im)

    def by_gather(k, first):
        row = jnp.broadcast_to(index_ref[0, k : k + 1, :], (8, LANES))
        lane, part = row & (LANES - 1), lax.shift_right_logical(row, 7)
        rows_here = slice(first, first + 8)
        re = im = 0
        for t in range(terms):
            partner = []
            for h in range(2):
                found = jnp.take_along_axis(spectra_ref[near[0], t, h, rows_here], lane, axis=1)
                for j in range(1, span):
                    other = jnp.take_along_axis(spectra_ref[near[j], t, h, rows_here], lane, axis=1)
                    found = jnp.where(part == j, other, found)
                partner.append(found)
            own_re = spectra_ref[block, t, 0, rows_here]
            own_im = spectra_ref[block, t, 1, rows_here]
            re = re + (own_re * partner[0] + own_im * partner[1])
            im = im + (own_im * partner[0] - own_re * partner[1])
        put(k, 0, rows_here, re)
        put(k, 1, rows_here, im)

    chunks = [range(k, min(k + 2, pairs - turned)) for k in range(0, pairs - turned, 2)]
    gathers = [(k, first) for k in range(pairs - turned, pairs) for first in range(0, rows, 8)]
    for n, ks in enumerate(chunks):
        by_product(n, ks)
        for k, first in gathers[n * len(gathers) // len(chunks) : (n + 1) * len(gathers) // len(chunks)]:
            by_gather(k, first)


def pair_products(spectra, index, groups, turned=6):
    blocks, terms, _, rows, _ = spectra.shape
    pairs = index.shape[1]
    reach = -(-REACH // LANES)
    shape = (groups, 2, rows, pairs // groups * LANES)
    return pl.pallas_call(
        functools.partial(pair_kernel, reach=reach, turned=turned),
        grid=(blocks,),
        in_specs=[
            pl.BlockSpec((1, pairs, LANES), lambda b: (b, 0, 0)),
            pl.BlockSpec(memory_space=pltpu.VMEM),
        ],
        out_specs=pl.BlockSpec((1, *shape), lambda b: (b, 0, 0, 0, 0)),
        out_shape=jax.ShapeDtypeStruct((blocks, *shape), jnp.float32),
        scratch_shapes=[
            pltpu.VMEM((blocks, 2, terms * 2 * rows, LANES), jnp.bfloat16),
            pltpu.VMEM((2, 2 * (2 * reach + 1) * LANES, 2 * LANES), jnp.bfloat16),
        ],
        compiler_params=pltpu.CompilerParams(vmem_limit_bytes=32 << 20),
    )(index, spectra)


def lag_kernel(cross_ref, high_ref, low_ref, out_ref):
    high, low = halves(cross_ref[...])
    total = dot_tn(high, low_ref[...]) + dot_tn(low, high_ref[...])
    out_ref[0] = total + dot_tn(high, high_ref[...])


def lag_transform(cross, table):
    count = cross.shape[1] // LANES
    high = table.astype(jnp.bfloat16)
    low = (table - high.astype(np.float32)).astype(jnp.bfloat16)
    return pl.pallas_call(
        lag_kernel,
        grid=(count,),
        in_specs=[
            pl.BlockSpec((2 * F, LANES), lambda i: (0, i)),
            pl.BlockSpec(memory_space=pltpu.VMEM),
            pl.BlockSpec(memory_space=pltpu.VMEM),
        ],
        out_specs=pl.BlockSpec((1, LANES, LAGS), lambda i: (i, 0, 0)),
        out_shape=jax.ShapeDtypeStruct((count, LANES, LAGS), jnp.float32),
        compiler_params=pltpu.CompilerParams(vmem_limit_bytes=32 << 20),
    )(cross, jnp.asarray(high), jnp.asarray(low))


def local(records, starts, offsets):
    axes = ("blk", "inner")
    blocks, groups = lax.axis_size("blk"), lax.axis_size("inner")
    devices = blocks * groups
    width = F // devices
    here, count = records.shape[:2]
    ids = jnp.arange(here, dtype=jnp.int32)[:, None] + REACH
    index = lax.all_gather((ids + offsets).T, "blk", axis=0)
    rows = max(width, 8)
    split = rows // width
    white = whiten(records, starts, rows)
    white = white.reshape(-1, count // split, split, 2, split, width, LANES)
    white = white.transpose(0, 4, 1, 3, 2, 5, 6).reshape(devices, -1, LANES)
    spectra = lax.all_to_all(white, axes, 0, 0, tiled=True)
    spectra = spectra.reshape(blocks, -1, 2, rows, LANES)
    cross = pair_products(spectra, index, groups)
    if split > 1:
        cross = cross.reshape(blocks, groups, 2, split, width, -1).sum(3)
    cross = lax.all_to_all(cross.reshape(devices, 2 * width, -1), axes, 0, 0, tiled=True)
    return lag_transform(cross.reshape(2 * F, -1), lag_table(width, count * groups))


def solution(mesh):
    placed = (P("blk", "inner", None), P("inner"), P("blk", None))
    return jax.shard_map(
        local, mesh=mesh, in_specs=placed, out_specs=P("inner", "blk", None), check_vma=False
    )
```

time: 160 us -> 147 us (0.919)
  Pallas kernels: 48.9 us -> 30.3 us
  local copies, waits for them, and re-layouts: 1.31 us -> 9.1 us
    pallas_call x2, Pallas kernels: 42.4 us -> 26 us  [the longest x1 20.7 us: pair_products(): pl.pallas_call(functools.partial(pair_kernel, reach=reach, turned=turned)...]
    unnamed x4 -> x22, local copies, waits for them, and re-layouts: 1.31 us -> 9.1 us
    pallas_call x1, Pallas kernels: 6.51 us -> 4.33 us  [lag_transform(): pl.pallas_call(lag_kernel, grid=(count,), in_specs=[pl.BlockSpec((2 * F,...]
where the time goes in v2:
time: 147 us
  blocking collectives  71.6 us (49%)
  Pallas kernels  30.3 us (21%)
  waiting for transfers between devices  28.6 us (19%)
  local copies, waits for them, and re-layouts  9.1 us (6%)
  starting transfers between devices  7.09 us (5%)
    all_to_all x1, blocking collectives, local(): lax.all_to_all(cross.reshape(devices, 2 * width, -1), axes, 0, 0, tiled=T...  52 us
    all_to_all x1, waiting for transfers between devices, local(): spectra = lax.all_to_all(white, axes, 0, 0, tiled=True)  28.6 us
    pallas_call x1, Pallas kernels, pair_products(): pl.pallas_call(functools.partial(pair_kernel, reach=reach, turned=turned)...  20.7 us
    all_gather x1, blocking collectives, local(): index = lax.all_gather((ids + offsets).T, 'blk', axis=0)  19.6 us
    unnamed x22, local copies, waits for them, and re-layouts  9.1 us
    all_to_all x1, starting transfers between devices, local(): spectra = lax.all_to_all(white, axes, 0, 0, tiled=True)  7.09 us
    pallas_call x1, Pallas kernels, whiten(): pl.pallas_call(whiten_kernel, grid=(here // part,), in_specs=[pl.BlockSpe...  5.29 us
    pallas_call x1, Pallas kernels, lag_transform(): pl.pallas_call(lag_kernel, grid=(count,), in_specs=[pl.BlockSpec((2 * F,...  4.33 us
  transfers between devices with their start and end apart: 1, of which 1 were waited for; matrix products, arithmetic and copies ran while one was open for 0% of the time, Pallas kernels for 0%

profile of v2, /device:TPU:1, one launch (start us, length us, event | category | flops | bytes accessed | tf_op | source)
XLA Modules:
  0.0 146.9 jit_solution(1984604293516346474)
XLA Ops:
  0.0 0.0 copy-start.1
  0.0 2.2 %copy-done.1 = f32[128,4,2048]{2,1,0:T(4,128)S(1)} copy-done((f32[128,4,2048]{2,1,0:T(4,128)S(1)}, f32[128,4,2048]{2,1,0:T(4,128)}, u32[]{:S(2)}) %copy-start.1) | copy-done | bytes 4194328
  2.2 0.0 copy-start.4
  2.2 1.2 copy-done.4
  3.4 0.0 copy-start.5
  3.4 1.0 copy-done.5
  4.5 0.9 copy-done.6
  5.4 0.9 copy-done.7
  6.4 0.8 copy-done.8
  7.1 0.7 copy-done.9
  7.8 5.3 %shard_map.100 = f32[32,4,2,16,128]{4,3,2,1,0:T(8,128)S(1)} custom-call(s32[4]{0:T(128)S(1)} %copy-done.9, f32[128,4,2048]{2,1,0:T(4,128)S(1)} %copy-done.1, f32[8,1024]{1,0:T(8,128)S(1)} %copy-done.8, f32[256,256]{1,0:T(8,128)S(1)} %copy-done.6, f32[256,256]{1,0:T(8,128)S(1)} %copy-done.7, f32[512,512]{1,0:T(8,128)S(1)} %copy-done.4, ...), custom_call_target="tpu_custom_call" | custom-call | tf_op jit(solution)/shard_map/pallas_call | solution.py:125
  13.1 0.0 copy-start
  13.1 1.3 copy-done
  14.4 7.1 %all-to-all-start = ((f32[32,128,128]{2,1,0:T(8,128)}), f32[32,128,128]{2,1,0:T(8,128)S(1)}, u32[]{:S(2)}, u32[]{:S(2)}) async-start(f32[32,128,128]{2,1,0:T(8,128)} %bitcast.10), calls=%async_computation | async-start | bytes 4194304 | tf_op jit(solution)/shard_map/all_to_all | solution.py:274
  21.5 0.0 copy-done.10
  21.5 19.6 %all-gather = s32[128,128]{1,0:T(8,128)S(1)} all-gather(s32[16,128]{1,0:T(8,128)S(1)} %add_bitcast_fusion), channel_id=2, replica_groups=mesh['blk'=8,'inner'=4] {'blk'}, dimensions={0}, use_global_device_ids=true | all-gather | bytes 73728 | tf_op jit(solution)/shard_map/all_gather | solution.py:268
  41.1 28.6 %all-to-all-done = f32[32,128,128]{2,1,0:T(8,128)S(1)} async-done(((f32[32,128,128]{2,1,0:T(8,128)}), f32[32,128,128]{2,1,0:T(8,128)S(1)}, u32[]{:S(2)}, u32[]{:S(2)}) %all-to-all-start) | async-done | bytes 2097184 | tf_op jit(solution)/shard_map/all_to_all | solution.py:274
  69.7 20.7 %shard_map.101 = f32[8,4,2,16,512]{4,3,2,1,0:T(8,128)S(1)} custom-call(s32[8,16,128]{2,1,0:T(8,128)S(1)} %bitcast.11, f32[8,16,2,16,128]{4,3,2,1,0:T(8,128)S(1)} %bitcast.7), custom_call_target="tpu_custom_call" | custom-call | tf_op jit(solution)/shard_map/pallas_call | solution.py:220
  90.5 0.0 copy-start.2
  90.5 0.0 copy-start.3
  90.5 52.0 %all_to_all.10 = f32[32,32,512]{2,1,0:T(8,128)S(1)} all-to-all(f32[32,32,512]{2,1,0:T(8,128)S(1)} %bitcast.9), channel_id=1, replica_groups=mesh['blk'=8,'inner'=4] {'blk','inner'}, dimensions={0} | all-to-all | bytes 4194304 | tf_op jit(solution)/shard_map/all_to_all | solution.py:279
  142.5 0.0 copy-done.2
  142.5 0.0 copy-done.3
  142.5 4.3 %shard_map.102 = f32[4,128,768]{2,1,0:T(8,128)} custom-call(f32[1024,512]{1,0:T(8,128)S(1)} %bitcast.8, bf16[1024,768]{1,0:T(8,128)(2,1)S(1)} %copy-done.2, bf16[1024,768]{1,0:T(8,128)(2,1)S(1)} %copy-done.3), custom_call_target="tpu_custom_call" | custom-call | tf_op jit(solution)/shard_map/pallas_call | solution.py:247
  (7 shorter events, 0.0 us)
Async XLA Ops:
  0.0 2.2 %copy-start.1 = (f32[128,4,2048]{2,1,0:T(4,128)S(1)}, f32[128,4,2048]{2,1,0:T(4,128)}, u32[]{:S(2)}) copy-start(f32[128,4,2048]{2,1,0:T(4,128)} %records_ref.1) | copy-start | bytes 12582916
  2.2 1.2 copy-start.4
  3.4 1.0 copy-start.5
  4.5 0.9 copy-start.6
  5.4 0.9 copy-start.7
  6.4 0.8 copy-start.8
  7.1 0.7 copy-start.9
  13.1 1.3 copy-start
  14.4 7.1 %copy-start.10 = (s32[128,16]{0,1:T(8,128)S(1)}, s32[128,16]{0,1:T(8,128)}, u32[]{:S(2)}) copy-start(s32[128,16]{0,1:T(8,128)} %param.12) | copy-start | bytes 24580
  14.4 55.3 %all-to-all-start = ((f32[32,128,128]{2,1,0:T(8,128)}), f32[32,128,128]{2,1,0:T(8,128)S(1)}, u32[]{:S(2)}, u32[]{:S(2)}) async-start(f32[32,128,128]{2,1,0:T(8,128)} %bitcast.10), calls=%async_computation | async-start | bytes 4194304 | tf_op jit(solution)/shard_map/all_to_all | solution.py:274
  90.5 52.1 %copy-start.2 = (bf16[1024,768]{1,0:T(8,128)(2,1)S(1)}, bf16[1024,768]{1,0:T(8,128)(2,1)}, u32[]{:S(2)}) copy-start(bf16[1024,768]{1,0:T(8,128)(2,1)} %constant.21.clone.high_ref) | copy-start | bytes 4718596
  90.5 52.1 %copy-start.3 = (bf16[1024,768]{1,0:T(8,128)(2,1)S(1)}, bf16[1024,768]{1,0:T(8,128)(2,1)}, u32[]{:S(2)}) copy-start(bf16[1024,768]{1,0:T(8,128)(2,1)} %constant.22.clone.low_ref) | copy-start | bytes 4718596

commit v3 on v2

--- a/solution.py
+++ b/solution.py
@@ -128,12 +128,12 @@
         in_specs=[
             pl.BlockSpec(memory_space=pltpu.SMEM),
             pl.BlockSpec((part, count, slot), lambda i: (i, 0, 0)),
-            *[pl.BlockSpec(memory_space=pltpu.VMEM) for _ in tables],
+            *[pl.BlockSpec(t.shape, lambda i: (0, 0)) for t in tables],
         ],
         out_specs=pl.BlockSpec(shape, lambda i: (0,) * 5),
         out_shape=jax.ShapeDtypeStruct(shape, jnp.float32),
         scratch_shapes=[pltpu.VMEM((count * LANES, SEG), jnp.float32)],
-        compiler_params=pltpu.CompilerParams(vmem_limit_bytes=32 << 20),
+        compiler_params=pltpu.CompilerParams(vmem_limit_bytes=56 << 20),
     )(starts, records, *tables)
 
 

time: 147 us -> 142 us (0.966)
  local copies, waits for them, and re-layouts: 9.1 us -> 0.02 us
  Pallas kernels: 30.3 us -> 34.2 us
    unnamed x22 -> x6, local copies, waits for them, and re-layouts: 9.1 us -> 0.02 us
    pallas_call x1, Pallas kernels: 5.29 us -> 9.12 us  [whiten(): pl.pallas_call(whiten_kernel, grid=(here // part,), in_specs=[pl.BlockSpe...]
where the time goes in v3:
time: 142 us
  blocking collectives  71.7 us (50%)
  Pallas kernels  34.2 us (24%)
  waiting for transfers between devices  28.6 us (20%)
  starting transfers between devices  7.09 us (5%)
    all_to_all x1, blocking collectives, local(): lax.all_to_all(cross.reshape(devices, 2 * width, -1), axes, 0, 0, tiled=T...  52 us
    all_to_all x1, waiting for transfers between devices, local(): spectra = lax.all_to_all(white, axes, 0, 0, tiled=True)  28.6 us
    pallas_call x1, Pallas kernels, pair_products(): pl.pallas_call(functools.partial(pair_kernel, reach=reach, turned=turned)...  20.7 us
    all_gather x1, blocking collectives, local(): index = lax.all_gather((ids + offsets).T, 'blk', axis=0)  19.6 us
    pallas_call x1, Pallas kernels, whiten(): pl.pallas_call(whiten_kernel, grid=(here // part,), in_specs=[pl.BlockSpe...  9.12 us
    all_to_all x1, starting transfers between devices, local(): spectra = lax.all_to_all(white, axes, 0, 0, tiled=True)  7.09 us
    pallas_call x1, Pallas kernels, lag_transform(): pl.pallas_call(lag_kernel, grid=(count,), in_specs=[pl.BlockSpec((2 * F,...  4.32 us
  transfers between devices with their start and end apart: 1, of which 1 were waited for; matrix products, arithmetic and copies ran while one was open for 0% of the time, Pallas kernels for 0%

profile of v3, /device:TPU:1, one launch (start us, length us, event | category | flops | bytes accessed | tf_op | source)
XLA Modules:
  0.0 141.6 jit_solution(14318161644667106578)
XLA Ops:
  0.0 9.1 %shard_map.100 = f32[32,4,2,16,128]{4,3,2,1,0:T(8,128)} custom-call(s32[4]{0:T(128)} %starts_ref.1, f32[128,4,2048]{2,1,0:T(4,128)} %records_ref.1, f32[8,1024]{1,0:T(8,128)} %constant.16.clone.hann_ref, f32[256,256]{1,0:T(8,128)} %constant.17.clone.even0_ref, f32[256,256]{1,0:T(8,128)} %constant.18.clone.even2_ref, f32[512,512]{1,0:T(8,128)} %constant.19.clone.odd_ref, ...), custom_call_target="tpu_custom_call" | custom-call | tf_op jit(solution)/shard_map/pallas_call | solution.py:125
  9.1 0.0 copy-start.2
  9.1 7.1 %all-to-all-start = ((f32[32,128,128]{2,1,0:T(8,128)}), f32[32,128,128]{2,1,0:T(8,128)S(1)}, u32[]{:S(2)}, u32[]{:S(2)}) async-start(f32[32,128,128]{2,1,0:T(8,128)} %bitcast.11), calls=%async_computation | async-start | bytes 4194304 | tf_op jit(solution)/shard_map/all_to_all | solution.py:274
  16.2 0.0 copy-done.2
  16.3 19.6 %all-gather = s32[128,128]{1,0:T(8,128)S(1)} all-gather(s32[16,128]{1,0:T(8,128)S(1)} %add_bitcast_fusion), channel_id=2, replica_groups=mesh['blk'=8,'inner'=4] {'blk'}, dimensions={0}, use_global_device_ids=true | all-gather | bytes 73728 | tf_op jit(solution)/shard_map/all_gather | solution.py:268
  35.9 28.6 %all-to-all-done = f32[32,128,128]{2,1,0:T(8,128)S(1)} async-done(((f32[32,128,128]{2,1,0:T(8,128)}), f32[32,128,128]{2,1,0:T(8,128)S(1)}, u32[]{:S(2)}, u32[]{:S(2)}) %all-to-all-start) | async-done | bytes 2097184 | tf_op jit(solution)/shard_map/all_to_all | solution.py:274
  64.5 20.7 %shard_map.101 = f32[8,4,2,16,512]{4,3,2,1,0:T(8,128)S(1)} custom-call(s32[8,16,128]{2,1,0:T(8,128)S(1)} %bitcast.10, f32[8,16,2,16,128]{4,3,2,1,0:T(8,128)S(1)} %bitcast.7), custom_call_target="tpu_custom_call" | custom-call | tf_op jit(solution)/shard_map/pallas_call | solution.py:220
  85.2 0.0 copy-start
  85.2 0.0 copy-start.1
  85.2 52.0 %all_to_all.10 = f32[32,32,512]{2,1,0:T(8,128)S(1)} all-to-all(f32[32,32,512]{2,1,0:T(8,128)S(1)} %bitcast.9), channel_id=1, replica_groups=mesh['blk'=8,'inner'=4] {'blk','inner'}, dimensions={0} | all-to-all | bytes 4194304 | tf_op jit(solution)/shard_map/all_to_all | solution.py:279
  137.3 0.0 copy-done
  137.3 0.0 copy-done.1
  137.3 4.3 %shard_map.102 = f32[4,128,768]{2,1,0:T(8,128)} custom-call(f32[1024,512]{1,0:T(8,128)S(1)} %bitcast.8, bf16[1024,768]{1,0:T(8,128)(2,1)S(1)} %copy-done, bf16[1024,768]{1,0:T(8,128)(2,1)S(1)} %copy-done.1), custom_call_target="tpu_custom_call" | custom-call | tf_op jit(solution)/shard_map/pallas_call | solution.py:247
  (2 shorter events, 0.0 us)
Async XLA Ops:
  9.1 7.1 %copy-start.2 = (s32[128,16]{0,1:T(8,128)S(1)}, s32[128,16]{0,1:T(8,128)}, u32[]{:S(2)}) copy-start(s32[128,16]{0,1:T(8,128)} %param.12) | copy-start | bytes 24580
  9.1 55.3 %all-to-all-start = ((f32[32,128,128]{2,1,0:T(8,128)}), f32[32,128,128]{2,1,0:T(8,128)S(1)}, u32[]{:S(2)}, u32[]{:S(2)}) async-start(f32[32,128,128]{2,1,0:T(8,128)} %bitcast.11), calls=%async_computation | async-start | bytes 4194304 | tf_op jit(solution)/shard_map/all_to_all | solution.py:274
  85.2 52.1 %copy-start = (bf16[1024,768]{1,0:T(8,128)(2,1)S(1)}, bf16[1024,768]{1,0:T(8,128)(2,1)}, u32[]{:S(2)}) copy-start(bf16[1024,768]{1,0:T(8,128)(2,1)} %constant.21.clone.high_ref) | copy-start | bytes 4718596
  85.2 52.1 %copy-start.1 = (bf16[1024,768]{1,0:T(8,128)(2,1)S(1)}, bf16[1024,768]{1,0:T(8,128)(2,1)}, u32[]{:S(2)}) copy-start(bf16[1024,768]{1,0:T(8,128)(2,1)} %constant.22.clone.low_ref) | copy-start | bytes 4718596

commit v4 on v3

v4 whole, which is shorter than its diff:
```python
import functools
import math

import jax
import jax.numpy as jnp
import numpy as np
from jax import lax
from jax.experimental import pallas as pl
from jax.experimental.pallas import tpu as pltpu
from jax.sharding import PartitionSpec as P

SEG = 1024
LAGS = 768
HALF = 32
REACH = 256
F = 512
LANES = 128
EPS = 1e-06


def bin_order():
    m = np.arange(128)
    return np.concatenate([4 * m, 4 * m + 2, 4 * m + 1, 4 * m[::-1] + 3])


def transform_tables():
    u = np.arange(256)

    def parts(bins, sign):
        angle = 2 * np.pi / SEG * (bins[:, None] * u[None, :] % SEG)
        return np.concatenate([np.cos(angle), sign * np.sin(angle)], 0).astype(np.float32)

    m = np.arange(256)
    return parts(4 * m[:128], -1), parts(4 * m[:128] + 2, -1), parts(4 * m + 1, 1)


def lag_tables(segment_count):
    bins = bin_order()[:, None]
    half = np.pi / SEG * bins * np.ones((1, LANES))
    angle = 2 * np.pi / SEG * bins * (np.arange(LAGS // 2)[None, :] + 0.5)
    factor = math.sqrt(segment_count / F) / segment_count
    tables = [np.cos(half).astype(np.float32), np.sin(half).astype(np.float32)]
    for table in (np.cos(angle) * factor, np.sin(angle) * factor):
        high = table.astype(jnp.bfloat16)
        tables += [high, (table - high.astype(np.float64)).astype(jnp.bfloat16)]
    return tables


def halves(x):
    high = x.astype(jnp.bfloat16)
    return high, (x - high.astype(jnp.float32)).astype(jnp.bfloat16)


def dot_nt(a, b, precision=None):
    return lax.dot_general(
        a, b, (((1,), (1,)), ((), ())), precision=precision, preferred_element_type=jnp.float32
    )


def dot_tn(a, b):
    return lax.dot_general(a, b, (((0,), (0,)), ((), ())), preferred_element_type=jnp.float32)


def hann_table():
    window = 0.5 - 0.5 * np.cos(2 * np.pi / SEG * np.arange(SEG))
    return np.tile(window[None, :], (8, 1)).astype(np.float32)


def whiten_kernel(
    starts_ref, records_ref, hann_ref, even0_ref, even2_ref, odd_ref, out_ref, folded_ref, band_ref, *, folds
):
    step = pl.program_id(0)
    part, count = records_ref.shape[:2]
    together, _, rows, _ = out_ref.shape[1:]
    columns = together * LANES

    @pl.when(step == 0)
    def _():
        def bins(axis):
            p = lax.broadcasted_iota(jnp.int32, (F, F), axis)
            even = jnp.where(p < 128, 4 * p, 4 * p - 510)
            return jnp.where(p < 256, even, jnp.where(p < 384, 4 * p - 1023, 2047 - 4 * p))

        distance = jnp.abs(bins(0) - bins(1))
        distance = jnp.minimum(distance, F - distance)
        band_ref[...] = jnp.where(distance <= HALF, 1.0, 0.0).astype(jnp.bfloat16)

    @pl.when(step < folds)
    def _():
        place = pl.multiple_of(step * part, part)
        samples = lax.broadcasted_iota(jnp.int32, (8, SEG), 1)
        for s in range(count):
            begin = starts_ref[s]
            window = pltpu.roll(hann_ref[...], lax.rem(begin, SEG), 1)[:1]
            early = jnp.where(samples >= begin, 1.0, 0.0)[:1] * window
            late = window - early
            x = records_ref[:, s, :SEG] * early + records_ref[:, s, SEG:] * late
            x = [x[:, 256 * j : 256 * (j + 1)] for j in range(4)]
            at = pl.ds(s * LANES + place, part)
            folded_ref[0, at, :] = (x[0] + x[2]) + (x[1] + x[3])
            folded_ref[1, at, :] = (x[0] + x[2]) - (x[1] + x[3])
            folded_ref[2, at, :] = x[0] - x[2]
            folded_ref[3, at, :] = x[1] - x[3]

    @pl.when(step >= folds)
    def _():
        at = pl.ds(pl.multiple_of((step - folds) * columns, columns), columns)
        highest = lax.Precision.HIGHEST
        s0 = dot_nt(even0_ref[...], folded_ref[0, at, :], highest)
        s2 = dot_nt(even2_ref[...], folded_ref[1, at, :], highest)
        odd = jnp.concatenate([folded_ref[2, at, :], folded_ref[3, at, :]], 0)
        s1 = dot_nt(odd_ref[...], odd, highest)
        s1_re = s1[:256, :columns] - s1[256:, columns:]
        s1_im = s1[256:, :columns] + s1[:256, columns:]
        re = jnp.concatenate([s0[:128], s2[:128], s1_re], 0)
        im = jnp.concatenate([s0[128:], s2[128:], -s1_im[:128], s1_im[128:]], 0)
        high, low = halves(re * re + im * im)
        smooth = jnp.dot(band_ref[...], high, preferred_element_type=jnp.float32)
        smooth += jnp.dot(band_ref[...], low, preferred_element_type=jnp.float32)
        scale = lax.rsqrt(smooth * (1.0 / (2 * HALF + 1)) + EPS)
        re, im = re * scale, im * scale
        for s in range(together):
            lanes = slice(s * LANES, (s + 1) * LANES)
            out_ref[:, s, 0] = re[:, lanes].reshape(-1, rows, LANES)
            out_ref[:, s, 1] = im[:, lanes].reshape(-1, rows, LANES)


def whiten(records, starts, rows):
    here, count, slot = records.shape
    part = 32
    folds = here // part
    together = 2 if count % 2 == 0 else 1
    tables = [jnp.asarray(t) for t in (hann_table(), *transform_tables())]
    return pl.pallas_call(
        functools.partial(whiten_kernel, folds=folds),
        grid=(folds + count // together,),
        in_specs=[
            pl.BlockSpec(memory_space=pltpu.SMEM),
            pl.BlockSpec((part, count, slot), lambda i: (jnp.minimum(i, folds - 1), 0, 0)),
            *[pl.BlockSpec(t.shape, lambda i: (0, 0)) for t in tables],
        ],
        out_specs=pl.BlockSpec(
            (F // rows, together, 2, rows, LANES), lambda i: (0, jnp.maximum(i - folds, 0), 0, 0, 0)
        ),
        out_shape=jax.ShapeDtypeStruct((F // rows, count, 2, rows, LANES), jnp.float32),
        scratch_shapes=[
            pltpu.VMEM((4, count * LANES, 256), jnp.float32),
            pltpu.VMEM((F, F), jnp.bfloat16),
        ],
        compiler_params=pltpu.CompilerParams(vmem_limit_bytes=56 << 20),
    )(starts, records, *tables)


def pair_kernel(index_ref, spectra_ref, out_ref, wide_ref, *, reach, turned):
    block = pl.program_id(0)
    blocks, terms, _, rows, _ = spectra_ref.shape
    pairs = index_ref.shape[1]
    groups = out_ref.shape[1]
    share = pairs // groups
    span = 2 * reach + 1

    @pl.when(block == 0)
    def _():
        def build(i, carry):
            wide_ref[i, 0], wide_ref[i, 1] = halves(spectra_ref[i].reshape(-1, LANES))
            return carry

        lax.fori_loop(0, blocks, build, 0)

    near = [lax.rem(block + (blocks - reach + j), blocks) for j in range(span)]
    left = jnp.concatenate([wide_ref[i, h] for i in near for h in range(2)], 1)
    ids = lax.broadcasted_iota(jnp.int32, (LANES, LANES), 0)

    def put(k, h, rows_here, x):
        z, q = k // share, k % share
        out_ref[0, z, h, rows_here, q * LANES : (q + 1) * LANES] = x

    def by_product(ks):
        hots = []
        for j in range(span):
            wanted = [index_ref[0, k : k + 1, :] - j * LANES for k in ks]
            hot = [jnp.where(ids == w, 1.0, 0.0).astype(jnp.bfloat16) for w in wanted]
            hot = jnp.concatenate(hot, 1)
            hots += [hot, hot]
        found = jnp.dot(left, jnp.concatenate(hots, 0), preferred_element_type=jnp.float32)
        found = found.reshape(terms, 2, rows, -1)
        for i, k in enumerate(ks):
            lanes = slice(i * LANES, (i + 1) * LANES)
            re = im = 0
            for t in range(terms):
                partner_re, partner_im = found[t, 0, :, lanes], found[t, 1, :, lanes]
                own_re, own_im = spectra_ref[block, t, 0], spectra_ref[block, t, 1]
                re = re + (own_re * partner_re + own_im * partner_im)
                im = im + (own_im * partner_re - own_re * partner_im)
            put(k, 0, slice(0, rows), re)
            put(k, 1, slice(0, rows), im)

    def by_gather(k, first):
        row = jnp.broadcast_to(index_ref[0, k : k + 1, :], (8, LANES))
        lane, part = row & (LANES - 1), lax.shift_right_logical(row, 7)
        rows_here = slice(first, first + 8)
        re = im = 0
        for t in range(terms):
            partner = []
            for h in range(2):
                found = jnp.take_along_axis(spectra_ref[near[0], t, h, rows_here], lane, axis=1)
                for j in range(1, span):
                    other = jnp.take_along_axis(spectra_ref[near[j], t, h, rows_here], lane, axis=1)
                    found = jnp.where(part == j, other, found)
                partner.append(found)
            own_re = spectra_ref[block, t, 0, rows_here]
            own_im = spectra_ref[block, t, 1, rows_here]
            re = re + (own_re * partner[0] + own_im * partner[1])
            im = im + (own_im * partner[0] - own_re * partner[1])
        put(k, 0, rows_here, re)
        put(k, 1, rows_here, im)

    chunks = [range(k, min(k + 2, pairs - turned)) for k in range(0, pairs - turned, 2)]
    gathers = [(k, first) for k in range(pairs - turned, pairs) for first in range(0, rows, 8)]
    for n, ks in enumerate(chunks):
        by_product(ks)
        for k, first in gathers[n * len(gathers) // len(chunks) : (n + 1) * len(gathers) // len(chunks)]:
            by_gather(k, first)


def pair_products(spectra, index, groups, turned=6):
    blocks, terms, _, rows, _ = spectra.shape
    pairs = index.shape[1]
    reach = -(-REACH // LANES)
    shape = (groups, 2, rows, pairs // groups * LANES)
    return pl.pallas_call(
        functools.partial(pair_kernel, reach=reach, turned=turned),
        grid=(blocks,),
        in_specs=[
            pl.BlockSpec((1, pairs, LANES), lambda b: (b, 0, 0)),
            pl.BlockSpec(memory_space=pltpu.VMEM),
        ],
        out_specs=pl.BlockSpec((1, *shape), lambda b: (b, 0, 0, 0, 0)),
        out_shape=jax.ShapeDtypeStruct((blocks, *shape), jnp.float32),
        scratch_shapes=[
            pltpu.VMEM((blocks, 2, terms * 2 * rows, LANES), jnp.bfloat16),
        ],
        compiler_params=pltpu.CompilerParams(vmem_limit_bytes=32 << 20),
    )(index, spectra)


def lag_kernel(cross_ref, turn_re_ref, turn_im_ref, even_ref, even_low_ref, odd_ref, odd_low_ref, out_ref):
    re = cross_ref[:, 0].reshape(F, LANES)
    im = cross_ref[:, 1].reshape(F, LANES)
    turn_re, turn_im = turn_re_ref[...], turn_im_ref[...]
    re, im = re * turn_re + im * turn_im, im * turn_re - re * turn_im

    def transform(x, high_ref, low_ref):
        high, low = halves(x)
        total = dot_tn(high, low_ref[...]) + dot_tn(low, high_ref[...])
        return total + dot_tn(high, high_ref[...])

    even = transform(re, even_ref, even_low_ref)
    odd = transform(im, odd_ref, odd_low_ref)
    half = LAGS // 2
    out_ref[0, :, half:] = even - odd
    before = even + odd
    mirror = LANES - 1 - lax.broadcasted_iota(jnp.int32, (LANES, LANES), 1)
    for first in range(0, half, LANES):
        turned = jnp.take_along_axis(before[:, first : first + LANES], mirror, axis=1)
        out_ref[0, :, half - first - LANES : half - first] = turned


def lag_transform(cross, tables):
    sources, _, width, columns = cross.shape
    return pl.pallas_call(
        lag_kernel,
        grid=(columns // LANES,),
        in_specs=[
            pl.BlockSpec((sources, 2, width, LANES), lambda i: (0, 0, 0, i)),
            *[pl.BlockSpec(memory_space=pltpu.VMEM) for _ in tables],
        ],
        out_specs=pl.BlockSpec((1, LANES, LAGS), lambda i: (i, 0, 0)),
        out_shape=jax.ShapeDtypeStruct((columns // LANES, LANES, LAGS), jnp.float32),
        compiler_params=pltpu.CompilerParams(vmem_limit_bytes=32 << 20),
    )(cross, *[jnp.asarray(t) for t in tables])


def local(records, starts, offsets):
    axes = ("blk", "inner")
    blocks, groups = lax.axis_size("blk"), lax.axis_size("inner")
    devices = blocks * groups
    width = F // devices
    here, count = records.shape[:2]
    ids = jnp.arange(here, dtype=jnp.int32)[:, None] + REACH
    index = lax.all_gather((ids + offsets).T, "blk", axis=0)
    rows = max(width, 8)
    split = rows // width
    white = whiten(records, starts, rows)
    white = white.reshape(-1, count // split, split, 2, split, width, LANES)
    white = white.transpose(0, 4, 1, 3, 2, 5, 6).reshape(devices, -1, LANES)
    spectra = lax.all_to_all(white, axes, 0, 0, tiled=True)
    spectra = spectra.reshape(blocks, -1, 2, rows, LANES)
    cross = pair_products(spectra, index, groups)
    if split > 1:
        cross = cross.reshape(blocks, groups, 2, split, width, -1).sum(3)
    cross = lax.all_to_all(cross.reshape(devices, 2 * width, -1), axes, 0, 0, tiled=True)
    cross = cross.reshape(devices, 2, width, -1)
    if split > 1:
        cross = cross.transpose(1, 0, 2, 3).reshape(1, 2, F, -1)
    return lag_transform(cross, lag_tables(count * groups))


def solution(mesh):
    placed = (P("blk", "inner", None), P("inner"), P("blk", None))
    return jax.shard_map(
        local, mesh=mesh, in_specs=placed, out_specs=P("inner", "blk", None), check_vma=False
    )
```

time: 142 us -> 142 us (level)
  no operation moved by 1% of the time
where the time goes in v4:
time: 142 us; the launch traced here: 141 us
  blocking collectives  71.7 us (50%)
  Pallas kernels  33.8 us (24%)
  waiting for transfers between devices  28.6 us (20%)
  starting transfers between devices  7.09 us (5%)
    all_to_all x1, blocking collectives, local(): lax.all_to_all(cross.reshape(devices, 2 * width, -1), axes, 0, 0, tiled=T...  52 us
    all_to_all x1, waiting for transfers between devices, local(): spectra = lax.all_to_all(white, axes, 0, 0, tiled=True)  28.6 us
    all_gather x1, blocking collectives, local(): index = lax.all_gather((ids + offsets).T, 'blk', axis=0)  19.6 us
    pallas_call x1, Pallas kernels, pair_products(): pl.pallas_call(functools.partial(pair_kernel, reach=reach, turned=turned)...  19.6 us
    pallas_call x1, Pallas kernels, whiten(): pl.pallas_call(functools.partial(whiten_kernel, folds=folds), grid=(folds...  10.2 us
    all_to_all x1, starting transfers between devices, local(): spectra = lax.all_to_all(white, axes, 0, 0, tiled=True)  7.09 us
    pallas_call x1, Pallas kernels, lag_transform(): pl.pallas_call(lag_kernel, grid=(columns // LANES,), in_specs=[pl.BlockSp...  3.96 us
  transfers between devices with their start and end apart: 1, of which 1 were waited for; matrix products, arithmetic and copies ran while one was open for 0% of the time, Pallas kernels for 0%

profile of v4, /device:TPU:1, one launch (start us, length us, event | category | flops | bytes accessed | tf_op | source)
XLA Modules:
  0.0 141.3 jit_solution(11704335097197029295)
XLA Ops:
  0.0 10.2 %shard_map.127 = f32[32,4,2,16,128]{4,3,2,1,0:T(8,128)} custom-call(s32[4]{0:T(128)} %starts_ref.1, f32[128,4,2048]{2,1,0:T(4,128)} %records_ref.1, f32[8,1024]{1,0:T(8,128)} %constant.22.clone.hann_ref, f32[256,256]{1,0:T(8,128)} %constant.23.clone.even0_ref, f32[256,256]{1,0:T(8,128)} %constant.24.clone.even2_ref, f32[512,256]{1,0:T(8,128)} %constant.25.clone.odd_ref), custom_call_target="tpu_custom_call" | custom-call | tf_op jit(solution)/shard_map/pallas_call | solution.py:134
  10.2 0.0 copy-start.6
  10.2 7.1 %all-to-all-start = ((f32[32,128,128]{2,1,0:T(8,128)}), f32[32,128,128]{2,1,0:T(8,128)S(1)}, u32[]{:S(2)}, u32[]{:S(2)}) async-start(f32[32,128,128]{2,1,0:T(8,128)} %bitcast.11), calls=%async_computation | async-start | bytes 4194304 | tf_op jit(solution)/shard_map/all_to_all | solution.py:297
  17.3 0.0 copy-done.6
  17.4 19.6 %all-gather = s32[128,128]{1,0:T(8,128)S(1)} all-gather(s32[16,128]{1,0:T(8,128)S(1)} %add_bitcast_fusion), channel_id=2, replica_groups=mesh['blk'=8,'inner'=4] {'blk'}, dimensions={0}, use_global_device_ids=true | all-gather | bytes 73728 | tf_op jit(solution)/shard_map/all_gather | solution.py:291
  37.0 28.6 %all-to-all-done = f32[32,128,128]{2,1,0:T(8,128)S(1)} async-done(((f32[32,128,128]{2,1,0:T(8,128)}), f32[32,128,128]{2,1,0:T(8,128)S(1)}, u32[]{:S(2)}, u32[]{:S(2)}) %all-to-all-start) | async-done | bytes 2097184 | tf_op jit(solution)/shard_map/all_to_all | solution.py:297
  65.6 19.6 %shard_map.128 = f32[8,4,2,16,512]{4,3,2,1,0:T(8,128)S(1)} custom-call(s32[8,16,128]{2,1,0:T(8,128)S(1)} %bitcast.10, f32[8,16,2,16,128]{4,3,2,1,0:T(8,128)S(1)} %bitcast.7), custom_call_target="tpu_custom_call" | custom-call | tf_op jit(solution)/shard_map/pallas_call | solution.py:231
  85.2 0.0 copy-start
  85.2 0.0 copy-start.1
  85.2 0.0 copy-start.2
  85.2 0.0 copy-start.3
  85.2 0.0 copy-start.4
  85.2 0.0 copy-start.5
  85.2 52.0 %all_to_all.10 = f32[32,32,512]{2,1,0:T(8,128)S(1)} all-to-all(f32[32,32,512]{2,1,0:T(8,128)S(1)} %bitcast.8), channel_id=1, replica_groups=mesh['blk'=8,'inner'=4] {'blk','inner'}, dimensions={0} | all-to-all | bytes 4194304 | tf_op jit(solution)/shard_map/all_to_all | solution.py:302
  137.3 0.0 copy-done
  137.3 0.0 copy-done.1
  137.3 0.0 copy-done.2
  137.3 0.0 copy-done.3
  137.3 0.0 copy-done.4
  137.3 0.0 copy-done.5
  137.3 4.0 %shard_map.129 = f32[4,128,768]{2,1,0:T(8,128)} custom-call(f32[32,2,16,512]{3,2,1,0:T(8,128)S(1)} %bitcast.9, f32[512,128]{1,0:T(8,128)S(1)} %copy-done.4, f32[512,128]{1,0:T(8,128)S(1)} %copy-done.5, bf16[512,384]{1,0:T(8,128)(2,1)S(1)} %copy-done, bf16[512,384]{1,0:T(8,128)(2,1)S(1)} %copy-done.1, bf16[512,384]{1,0:T(8,128)(2,1)S(1)} %copy-done.2, ...), custom_call_target="tpu_custom_call" | custom-call | tf_op jit(solution)/shard_map/pallas_call | solution.py:271
  (2 shorter events, 0.0 us)
Async XLA Ops:
  10.2 7.1 %copy-start.6 = (s32[128,16]{0,1:T(8,128)S(1)}, s32[128,16]{0,1:T(8,128)}, u32[]{:S(2)}) copy-start(s32[128,16]{0,1:T(8,128)} %param.15) | copy-start | bytes 24580
  10.2 55.3 %all-to-all-start = ((f32[32,128,128]{2,1,0:T(8,128)}), f32[32,128,128]{2,1,0:T(8,128)S(1)}, u32[]{:S(2)}, u32[]{:S(2)}) async-start(f32[32,128,128]{2,1,0:T(8,128)} %bitcast.11), calls=%async_computation | async-start | bytes 4194304 | tf_op jit(solution)/shard_map/all_to_all | solution.py:297
  85.2 52.1 %copy-start = (bf16[512,384]{1,0:T(8,128)(2,1)S(1)}, bf16[512,384]{1,0:T(8,128)(2,1)}, u32[]{:S(2)}) copy-start(bf16[512,384]{1,0:T(8,128)(2,1)} %constant.28.clone.even_ref) | copy-start | bytes 1179652
  85.2 52.1 %copy-start.1 = (bf16[512,384]{1,0:T(8,128)(2,1)S(1)}, bf16[512,384]{1,0:T(8,128)(2,1)}, u32[]{:S(2)}) copy-start(bf16[512,384]{1,0:T(8,128)(2,1)} %constant.29.clone.even_low_ref) | copy-start | bytes 1179652
  85.2 52.1 %copy-start.2 = (bf16[512,384]{1,0:T(8,128)(2,1)S(1)}, bf16[512,384]{1,0:T(8,128)(2,1)}, u32[]{:S(2)}) copy-start(bf16[512,384]{1,0:T(8,128)(2,1)} %constant.30.clone.odd_ref) | copy-start | bytes 1179652
  85.2 52.1 %copy-start.3 = (bf16[512,384]{1,0:T(8,128)(2,1)S(1)}, bf16[512,384]{1,0:T(8,128)(2,1)}, u32[]{:S(2)}) copy-start(bf16[512,384]{1,0:T(8,128)(2,1)} %constant.31.clone.odd_low_ref) | copy-start | bytes 1179652
  85.2 52.1 %copy-start.4 = (f32[512,128]{1,0:T(8,128)S(1)}, f32[512,128]{1,0:T(8,128)}, u32[]{:S(2)}) copy-start(f32[512,128]{1,0:T(8,128)} %constant.26.clone.turn_re_ref) | copy-start | bytes 786436
  85.2 52.1 %copy-start.5 = (f32[512,128]{1,0:T(8,128)S(1)}, f32[512,128]{1,0:T(8,128)}, u32[]{:S(2)}) copy-start(f32[512,128]{1,0:T(8,128)} %constant.27.clone.turn_im_ref) | copy-start | bytes 786436

commit v5 on v4

--- a/solution.py
+++ b/solution.py
@@ -67,45 +67,61 @@
 
 
 def whiten_kernel(
-    starts_ref, records_ref, hann_ref, even0_ref, even2_ref, odd_ref, out_ref, folded_ref, band_ref, *, folds
+    starts_ref, records_hbm, hann_hbm, even0_hbm, even2_hbm, odd_hbm, out_hbm,
+    records_ref, hann_ref, even0_ref, even2_ref, odd_ref, folded_ref, band_ref, out_ref,
+    table_sems, record_sems, out_sems,
 ):
-    step = pl.program_id(0)
-    part, count = records_ref.shape[:2]
-    together, _, rows, _ = out_ref.shape[1:]
+    here, count = records_ref.shape[:2]
+    rows = out_ref.shape[4]
+    parts, halves_out = record_sems.shape[0], out_sems.shape[0]
+    part, together = here // parts, count // halves_out
     columns = together * LANES
 
-    @pl.when(step == 0)
-    def _():
-        def bins(axis):
-            p = lax.broadcasted_iota(jnp.int32, (F, F), axis)
-            even = jnp.where(p < 128, 4 * p, 4 * p - 510)
-            return jnp.where(p < 256, even, jnp.where(p < 384, 4 * p - 1023, 2047 - 4 * p))
-
-        distance = jnp.abs(bins(0) - bins(1))
-        distance = jnp.minimum(distance, F - distance)
-        band_ref[...] = jnp.where(distance <= HALF, 1.0, 0.0).astype(jnp.bfloat16)
-
-    @pl.when(step < folds)
-    def _():
-        place = pl.multiple_of(step * part, part)
-        samples = lax.broadcasted_iota(jnp.int32, (8, SEG), 1)
-        for s in range(count):
-            begin = starts_ref[s]
-            window = pltpu.roll(hann_ref[...], lax.rem(begin, SEG), 1)[:1]
-            early = jnp.where(samples >= begin, 1.0, 0.0)[:1] * window
-            late = window - early
-            x = records_ref[:, s, :SEG] * early + records_ref[:, s, SEG:] * late
+    tables = [(hann_hbm, hann_ref), (even0_hbm, even0_ref), (even2_hbm, even2_ref), (odd_hbm, odd_ref)]
+    tables = [pltpu.make_async_copy(s, d, table_sems.at[i]) for i, (s, d) in enumerate(tables)]
+    pieces = [pl.ds(p * part, part) for p in range(parts)]
+    pieces = [
+        pltpu.make_async_copy(records_hbm.at[at], records_ref.at[at], record_sems.at[p])
+        for p, at in enumerate(pieces)
+    ]
+    for copy in [tables[0], *pieces, *tables[1:]]:
+        copy.start()
+
+    def bins(axis):
+        p = lax.broadcasted_iota(jnp.int32, (F, F), axis)
+        even = jnp.where(p < 128, 4 * p, 4 * p - 510)
+        return jnp.where(p < 256, even, jnp.where(p < 384, 4 * p - 1023, 2047 - 4 * p))
+
+    distance = jnp.abs(bins(0) - bins(1))
+    distance = jnp.minimum(distance, F - distance)
+    band_ref[...] = jnp.where(distance <= HALF, 1.0, 0.0).astype(jnp.bfloat16)
+
+    samples = lax.broadcasted_iota(jnp.int32, (8, SEG), 1)
+    tables[0].wait()
+    windows = []
+    for s in range(count):
+        begin = starts_ref[s]
+        window = pltpu.roll(hann_ref[...], lax.rem(begin, SEG), 1)[:1]
+        early = jnp.where(samples >= begin, 1.0, 0.0)[:1] * window
+        windows.append((early, window - early))
+    for p, copy in enumerate(pieces):
+        copy.wait()
+        for s, (early, late) in enumerate(windows):
+            at = slice(p * part, (p + 1) * part)
+            x = records_ref[at, s, :SEG] * early + records_ref[at, s, SEG:] * late
             x = [x[:, 256 * j : 256 * (j + 1)] for j in range(4)]
-            at = pl.ds(s * LANES + place, part)
+            at = slice(s * LANES + p * part, s * LANES + (p + 1) * part)
             folded_ref[0, at, :] = (x[0] + x[2]) + (x[1] + x[3])
             folded_ref[1, at, :] = (x[0] + x[2]) - (x[1] + x[3])
             folded_ref[2, at, :] = x[0] - x[2]
             folded_ref[3, at, :] = x[1] - x[3]
 
-    @pl.when(step >= folds)
-    def _():
-        at = pl.ds(pl.multiple_of((step - folds) * columns, columns), columns)
-        highest = lax.Precision.HIGHEST
+    for copy in tables[1:]:
+        copy.wait()
+    highest = lax.Precision.HIGHEST
+    done = []
+    for n in range(halves_out):
+        at = slice(n * columns, (n + 1) * columns)
         s0 = dot_nt(even0_ref[...], folded_ref[0, at, :], highest)
         s2 = dot_nt(even2_ref[...], folded_ref[1, at, :], highest)
         odd = jnp.concatenate([folded_ref[2, at, :], folded_ref[3, at, :]], 0)
@@ -121,64 +137,76 @@
         re, im = re * scale, im * scale
         for s in range(together):
             lanes = slice(s * LANES, (s + 1) * LANES)
-            out_ref[:, s, 0] = re[:, lanes].reshape(-1, rows, LANES)
-            out_ref[:, s, 1] = im[:, lanes].reshape(-1, rows, LANES)
+            out_ref[n, :, s, 0] = re[:, lanes].reshape(-1, rows, LANES)
+            out_ref[n, :, s, 1] = im[:, lanes].reshape(-1, rows, LANES)
+        segments = pl.ds(n * together, together)
+        done.append(pltpu.make_async_copy(out_ref.at[n], out_hbm.at[:, segments], out_sems.at[n]))
+        done[n].start()
+    for copy in done:
+        copy.wait()
 
 
 def whiten(records, starts, rows):
-    here, count, slot = records.shape
-    part = 32
-    folds = here // part
-    together = 2 if count % 2 == 0 else 1
+    count = records.shape[1]
+    parts = 4
+    splits = 2 if count % 2 == 0 else 1
     tables = [jnp.asarray(t) for t in (hann_table(), *transform_tables())]
     return pl.pallas_call(
-        functools.partial(whiten_kernel, folds=folds),
-        grid=(folds + count // together,),
+        whiten_kernel,
         in_specs=[
             pl.BlockSpec(memory_space=pltpu.SMEM),
-            pl.BlockSpec((part, count, slot), lambda i: (jnp.minimum(i, folds - 1), 0, 0)),
-            *[pl.BlockSpec(t.shape, lambda i: (0, 0)) for t in tables],
+            *[pl.BlockSpec(memory_space=pl.ANY) for _ in range(1 + len(tables))],
         ],
-        out_specs=pl.BlockSpec(
-            (F // rows, together, 2, rows, LANES), lambda i: (0, jnp.maximum(i - folds, 0), 0, 0, 0)
-        ),
+        out_specs=pl.BlockSpec(memory_space=pl.ANY),
         out_shape=jax.ShapeDtypeStruct((F // rows, count, 2, rows, LANES), jnp.float32),
         scratch_shapes=[
+            pltpu.VMEM(records.shape, jnp.float32),
+            *[pltpu.VMEM(t.shape, jnp.float32) for t in tables],
             pltpu.VMEM((4, count * LANES, 256), jnp.float32),
             pltpu.VMEM((F, F), jnp.bfloat16),
+            pltpu.VMEM((splits, F // rows, count // splits, 2, rows, LANES), jnp.float32),
+            pltpu.SemaphoreType.DMA((len(tables),)),
+            pltpu.SemaphoreType.DMA((parts,)),
+            pltpu.SemaphoreType.DMA((splits,)),
         ],
         compiler_params=pltpu.CompilerParams(vmem_limit_bytes=56 << 20),
     )(starts, records, *tables)
 
 
 def pair_kernel(index_ref, spectra_ref, out_ref, wide_ref, *, reach, turned):
-    block = pl.program_id(0)
+    blocks, terms, _, rows, _ = spectra_ref.shape
+
+    def build(i, carry):
+        wide_ref[i, 0], wide_ref[i, 1] = halves(spectra_ref[i].reshape(-1, LANES))
+        return carry
+
+    lax.fori_loop(0, blocks, build, 0)
+    ids = lax.broadcasted_iota(jnp.int32, (LANES, LANES), 0)
+
+    def one_block(block, carry):
+        pair_block(block, index_ref, spectra_ref, out_ref, wide_ref, ids, reach, turned)
+        return carry
+
+    lax.fori_loop(0, blocks, one_block, 0)
+
+
+def pair_block(block, index_ref, spectra_ref, out_ref, wide_ref, ids, reach, turned):
     blocks, terms, _, rows, _ = spectra_ref.shape
     pairs = index_ref.shape[1]
     groups = out_ref.shape[1]
     share = pairs // groups
     span = 2 * reach + 1
-
-    @pl.when(block == 0)
-    def _():
-        def build(i, carry):
-            wide_ref[i, 0], wide_ref[i, 1] = halves(spectra_ref[i].reshape(-1, LANES))
-            return carry
-
-        lax.fori_loop(0, blocks, build, 0)
-
     near = [lax.rem(block + (blocks - reach + j), blocks) for j in range(span)]
     left = jnp.concatenate([wide_ref[i, h] for i in near for h in range(2)], 1)
-    ids = lax.broadcasted_iota(jnp.int32, (LANES, LANES), 0)
 
     def put(k, h, rows_here, x):
         z, q = k // share, k % share
-        out_ref[0, z, h, rows_here, q * LANES : (q + 1) * LANES] = x
+        out_ref[block, z, h, rows_here, q * LANES : (q + 1) * LANES] = x
 
     def by_product(ks):
         hots = []
         for j in range(span):
-            wanted = [index_ref[0, k : k + 1, :] - j * LANES for k in ks]
+            wanted = [index_ref[block, k : k + 1, :] - j * LANES for k in ks]
             hot = [jnp.where(ids == w, 1.0, 0.0).astype(jnp.bfloat16) for w in wanted]
             hot = jnp.concatenate(hot, 1)
             hots += [hot, hot]
@@ -196,7 +224,7 @@
             put(k, 1, slice(0, rows), im)
 
     def by_gather(k, first):
-        row = jnp.broadcast_to(index_ref[0, k : k + 1, :], (8, LANES))
+        row = jnp.broadcast_to(index_ref[block, k : k + 1, :], (8, LANES))
         lane, part = row & (LANES - 1), lax.shift_right_logical(row, 7)
         rows_here = slice(first, first + 8)
         re = im = 0
@@ -230,12 +258,8 @@
     shape = (groups, 2, rows, pairs // groups * LANES)
     return pl.pallas_call(
         functools.partial(pair_kernel, reach=reach, turned=turned),
-        grid=(blocks,),
-        in_specs=[
-            pl.BlockSpec((1, pairs, LANES), lambda b: (b, 0, 0)),
-            pl.BlockSpec(memory_space=pltpu.VMEM),
-        ],
-        out_specs=pl.BlockSpec((1, *shape), lambda b: (b, 0, 0, 0, 0)),
+        in_specs=[pl.BlockSpec(memory_space=pltpu.VMEM)] * 2,
+        out_specs=pl.BlockSpec(memory_space=pltpu.VMEM),
         out_shape=jax.ShapeDtypeStruct((blocks, *shape), jnp.float32),
         scratch_shapes=[
             pltpu.VMEM((blocks, 2, terms * 2 * rows, LANES), jnp.bfloat16),
@@ -244,39 +268,46 @@
     )(index, spectra)
 
 
-def lag_kernel(cross_ref, turn_re_ref, turn_im_ref, even_ref, even_low_ref, odd_ref, odd_low_ref, out_ref):
-    re = cross_ref[:, 0].reshape(F, LANES)
-    im = cross_ref[:, 1].reshape(F, LANES)
+def lag_kernel(cross_ref, turn_re_ref, turn_im_ref, even_ref, even_low_ref, odd_ref, odd_low_ref, out_hbm, out_ref, sems):
     turn_re, turn_im = turn_re_ref[...], turn_im_ref[...]
-    re, im = re * turn_re + im * turn_im, im * turn_re - re * turn_im
+    half = LAGS // 2
+    mirror = LANES - 1 - lax.broadcasted_iota(jnp.int32, (LANES, LANES), 1)
 
     def transform(x, high_ref, low_ref):
         high, low = halves(x)
         total = dot_tn(high, low_ref[...]) + dot_tn(low, high_ref[...])
         return total + dot_tn(high, high_ref[...])
 
-    even = transform(re, even_ref, even_low_ref)
-    odd = transform(im, odd_ref, odd_low_ref)
-    half = LAGS // 2
-    out_ref[0, :, half:] = even - odd
-    before = even + odd
-    mirror = LANES - 1 - lax.broadcasted_iota(jnp.int32, (LANES, LANES), 1)
-    for first in range(0, half, LANES):
-        turned = jnp.take_along_axis(before[:, first : first + LANES], mirror, axis=1)
-        out_ref[0, :, half - first - LANES : half - first] = turned
+    done = []
+    for i in range(out_ref.shape[0]):
+        lanes = slice(i * LANES, (i + 1) * LANES)
+        re = cross_ref[:, 0, :, lanes].reshape(F, LANES)
+        im = cross_ref[:, 1, :, lanes].reshape(F, LANES)
+        re, im = re * turn_re + im * turn_im, im * turn_re - re * turn_im
+        even = transform(re, even_ref, even_low_ref)
+        odd = transform(im, odd_ref, odd_low_ref)
+        out_ref[i, :, half:] = even - odd
+        before = even + odd
+        for first in range(0, half, LANES):
+            turned = jnp.take_along_axis(before[:, first : first + LANES], mirror, axis=1)
+            out_ref[i, :, half - first - LANES : half - first] = turned
+        done.append(pltpu.make_async_copy(out_ref.at[i], out_hbm.at[i], sems.at[i]))
+        done[i].start()
+    for copy in done:
+        copy.wait()
 
 
 def lag_transform(cross, tables):
-    sources, _, width, columns = cross.shape
+    count = cross.shape[3] // LANES
     return pl.pallas_call(
         lag_kernel,
-        grid=(columns // LANES,),
-        in_specs=[
-            pl.BlockSpec((sources, 2, width, LANES), lambda i: (0, 0, 0, i)),
-            *[pl.BlockSpec(memory_space=pltpu.VMEM) for _ in tables],
+        in_specs=[pl.BlockSpec(memory_space=pltpu.VMEM)] * (1 + len(tables)),
+        out_specs=pl.BlockSpec(memory_space=pl.ANY),
+        out_shape=jax.ShapeDtypeStruct((count, LANES, LAGS), jnp.float32),
+        scratch_shapes=[
+            pltpu.VMEM((count, LANES, LAGS), jnp.float32),
+            pltpu.SemaphoreType.DMA((count,)),
         ],
-        out_specs=pl.BlockSpec((1, LANES, LAGS), lambda i: (i, 0, 0)),
-        out_shape=jax.ShapeDtypeStruct((columns // LANES, LANES, LAGS), jnp.float32),
         compiler_params=pltpu.CompilerParams(vmem_limit_bytes=32 << 20),
     )(cross, *[jnp.asarray(t) for t in tables])
 

time: 142 us -> 140 us (0.986)
  no operation moved by 1% of the time
where the time goes in v5:
time: 140 us
  blocking collectives  71.7 us (51%)
  Pallas kernels  32.4 us (23%)
  waiting for transfers between devices  28.6 us (20%)
  starting transfers between devices  7.1 us (5%)
    all_to_all x1, blocking collectives, local(): lax.all_to_all(cross.reshape(devices, 2 * width, -1), axes, 0, 0, tiled=T...  52.1 us
    all_to_all x1, waiting for transfers between devices, local(): spectra = lax.all_to_all(white, axes, 0, 0, tiled=True)  28.6 us
    all_gather x1, blocking collectives, local(): index = lax.all_gather((ids + offsets).T, 'blk', axis=0)  19.6 us
    pallas_call x1, Pallas kernels, pair_products(): pl.pallas_call(functools.partial(pair_kernel, reach=reach, turned=turned)...  19.3 us
    pallas_call x1, Pallas kernels, whiten(): pl.pallas_call(whiten_kernel, in_specs=[pl.BlockSpec(memory_space=pltpu.S...  9.94 us
    all_to_all x1, starting transfers between devices, local(): spectra = lax.all_to_all(white, axes, 0, 0, tiled=True)  7.1 us
    pallas_call x1, Pallas kernels, lag_transform(): pl.pallas_call(lag_kernel, in_specs=[pl.BlockSpec(memory_space=pltpu.VMEM...  3.1 us
  transfers between devices with their start and end apart: 1, of which 1 were waited for; matrix products, arithmetic and copies ran while one was open for 0% of the time, Pallas kernels for 0%

profile of v5, /device:TPU:1, one launch (start us, length us, event | category | flops | bytes accessed | tf_op | source)
XLA Modules:
  0.0 139.9 jit_solution(16996274794417535481)
XLA Ops:
  0.0 9.9 %shard_map.127 = f32[32,4,2,16,128]{4,3,2,1,0:T(8,128)} custom-call(s32[4]{0:T(128)} %starts_ref.1, f32[128,4,2048]{2,1,0:T(4,128)} %records_hbm.1, f32[8,1024]{1,0:T(8,128)} %constant.22.clone.hann_hbm, f32[256,256]{1,0:T(8,128)} %constant.23.clone.even0_hbm, f32[256,256]{1,0:T(8,128)} %constant.24.clone.even2_hbm, f32[512,256]{1,0:T(8,128)} %constant.25.clone.odd_hbm), custom_call_target="tpu_custom_call" | custom-call | tf_op jit(solution)/shard_map/pallas_call | solution.py:154
  10.0 0.0 copy-start.6
  10.0 7.1 %all-to-all-start = ((f32[32,128,128]{2,1,0:T(8,128)}), f32[32,128,128]{2,1,0:T(8,128)S(1)}, u32[]{:S(2)}, u32[]{:S(2)}) async-start(f32[32,128,128]{2,1,0:T(8,128)} %bitcast.11), calls=%async_computation | async-start | bytes 4194304 | tf_op jit(solution)/shard_map/all_to_all | solution.py:328
  17.1 0.0 copy-done.6
  17.1 19.6 %all-gather = s32[128,128]{1,0:T(8,128)S(1)} all-gather(s32[16,128]{1,0:T(8,128)S(1)} %add_bitcast_fusion), channel_id=2, replica_groups=mesh['blk'=8,'inner'=4] {'blk'}, dimensions={0}, use_global_device_ids=true | all-gather | bytes 73728 | tf_op jit(solution)/shard_map/all_gather | solution.py:322
  36.7 28.6 %all-to-all-done = f32[32,128,128]{2,1,0:T(8,128)S(1)} async-done(((f32[32,128,128]{2,1,0:T(8,128)}), f32[32,128,128]{2,1,0:T(8,128)S(1)}, u32[]{:S(2)}, u32[]{:S(2)}) %all-to-all-start) | async-done | bytes 2097184 | tf_op jit(solution)/shard_map/all_to_all | solution.py:328
  65.3 19.3 %shard_map.128 = f32[8,4,2,16,512]{4,3,2,1,0:T(8,128)S(1)} custom-call(s32[8,16,128]{2,1,0:T(8,128)S(1)} %bitcast.10, f32[8,16,2,16,128]{4,3,2,1,0:T(8,128)S(1)} %bitcast.7), custom_call_target="tpu_custom_call" | custom-call | tf_op jit(solution)/shard_map/pallas_call | solution.py:259
  84.6 0.0 copy-start
  84.7 0.0 copy-start.1
  84.7 0.0 copy-start.2
  84.7 0.0 copy-start.3
  84.7 0.0 copy-start.4
  84.7 0.0 copy-start.5
  84.7 52.1 %all_to_all.10 = f32[32,32,512]{2,1,0:T(8,128)S(1)} all-to-all(f32[32,32,512]{2,1,0:T(8,128)S(1)} %bitcast.8), channel_id=1, replica_groups=mesh['blk'=8,'inner'=4] {'blk','inner'}, dimensions={0} | all-to-all | bytes 4194304 | tf_op jit(solution)/shard_map/all_to_all | solution.py:333
  136.8 0.0 copy-done
  136.8 0.0 copy-done.1
  136.8 0.0 copy-done.2
  136.8 0.0 copy-done.3
  136.8 0.0 copy-done.4
  136.8 0.0 copy-done.5
  136.8 3.1 %shard_map.129 = f32[4,128,768]{2,1,0:T(8,128)} custom-call(f32[32,2,16,512]{3,2,1,0:T(8,128)S(1)} %bitcast.9, f32[512,128]{1,0:T(8,128)S(1)} %copy-done.4, f32[512,128]{1,0:T(8,128)S(1)} %copy-done.5, bf16[512,384]{1,0:T(8,128)(2,1)S(1)} %copy-done, bf16[512,384]{1,0:T(8,128)(2,1)S(1)} %copy-done.1, bf16[512,384]{1,0:T(8,128)(2,1)S(1)} %copy-done.2, ...), custom_call_target="tpu_custom_call" | custom-call | tf_op jit(solution)/shard_map/pallas_call | solution.py:302
  (2 shorter events, 0.0 us)
Async XLA Ops:
  10.0 7.1 %copy-start.6 = (s32[128,16]{0,1:T(8,128)S(1)}, s32[128,16]{0,1:T(8,128)}, u32[]{:S(2)}) copy-start(s32[128,16]{0,1:T(8,128)} %param.15) | copy-start | bytes 24580
  10.0 55.4 %all-to-all-start = ((f32[32,128,128]{2,1,0:T(8,128)}), f32[32,128,128]{2,1,0:T(8,128)S(1)}, u32[]{:S(2)}, u32[]{:S(2)}) async-start(f32[32,128,128]{2,1,0:T(8,128)} %bitcast.11), calls=%async_computation | async-start | bytes 4194304 | tf_op jit(solution)/shard_map/all_to_all | solution.py:328
  84.6 52.1 %copy-start = (bf16[512,384]{1,0:T(8,128)(2,1)S(1)}, bf16[512,384]{1,0:T(8,128)(2,1)}, u32[]{:S(2)}) copy-start(bf16[512,384]{1,0:T(8,128)(2,1)} %constant.28.clone.even_ref) | copy-start | bytes 1179652
  84.7 52.1 %copy-start.1 = (bf16[512,384]{1,0:T(8,128)(2,1)S(1)}, bf16[512,384]{1,0:T(8,128)(2,1)}, u32[]{:S(2)}) copy-start(bf16[512,384]{1,0:T(8,128)(2,1)} %constant.29.clone.even_low_ref) | copy-start | bytes 1179652
  84.7 52.1 %copy-start.2 = (bf16[512,384]{1,0:T(8,128)(2,1)S(1)}, bf16[512,384]{1,0:T(8,128)(2,1)}, u32[]{:S(2)}) copy-start(bf16[512,384]{1,0:T(8,128)(2,1)} %constant.30.clone.odd_ref) | copy-start | bytes 1179652
  84.7 52.1 %copy-start.3 = (bf16[512,384]{1,0:T(8,128)(2,1)S(1)}, bf16[512,384]{1,0:T(8,128)(2,1)}, u32[]{:S(2)}) copy-start(bf16[512,384]{1,0:T(8,128)(2,1)} %constant.31.clone.odd_low_ref) | copy-start | bytes 1179652
  84.7 52.1 %copy-start.4 = (f32[512,128]{1,0:T(8,128)S(1)}, f32[512,128]{1,0:T(8,128)}, u32[]{:S(2)}) copy-start(f32[512,128]{1,0:T(8,128)} %constant.26.clone.turn_re_ref) | copy-start | bytes 786436
  84.7 52.1 %copy-start.5 = (f32[512,128]{1,0:T(8,128)S(1)}, f32[512,128]{1,0:T(8,128)}, u32[]{:S(2)}) copy-start(f32[512,128]{1,0:T(8,128)} %constant.27.clone.turn_im_ref) | copy-start | bytes 786436

commit v6 on v5

--- a/solution.py
+++ b/solution.py
@@ -67,13 +67,13 @@
 
 
 def whiten_kernel(
-    starts_ref, records_hbm, hann_hbm, even0_hbm, even2_hbm, odd_hbm, out_hbm,
-    records_ref, hann_ref, even0_ref, even2_ref, odd_ref, folded_ref, band_ref, out_ref,
-    table_sems, record_sems, out_sems,
+    starts_ref, records_hbm, hann_hbm, even0_hbm, even2_hbm, odd_hbm, *rest
 ):
+    *outs_hbm, records_ref, hann_ref, even0_ref, even2_ref, odd_ref, folded_ref, band_ref = rest[:-4]
+    out_ref, table_sems, record_sems, out_sems = rest[-4:]
     here, count = records_ref.shape[:2]
-    rows = out_ref.shape[4]
-    parts, halves_out = record_sems.shape[0], out_sems.shape[0]
+    rows = out_ref.shape[5]
+    parts, (halves_out, chunks) = record_sems.shape[0], out_sems.shape
     part, together = here // parts, count // halves_out
     columns = together * LANES
 
@@ -135,21 +135,25 @@
         smooth += jnp.dot(band_ref[...], low, preferred_element_type=jnp.float32)
         scale = lax.rsqrt(smooth * (1.0 / (2 * HALF + 1)) + EPS)
         re, im = re * scale, im * scale
-        for s in range(together):
-            lanes = slice(s * LANES, (s + 1) * LANES)
-            out_ref[n, :, s, 0] = re[:, lanes].reshape(-1, rows, LANES)
-            out_ref[n, :, s, 1] = im[:, lanes].reshape(-1, rows, LANES)
         segments = pl.ds(n * together, together)
-        done.append(pltpu.make_async_copy(out_ref.at[n], out_hbm.at[:, segments], out_sems.at[n]))
-        done[n].start()
+        for c, out_hbm in enumerate(outs_hbm):
+            mine = slice(c * F // chunks, (c + 1) * F // chunks)
+            for s in range(together):
+                lanes = slice(s * LANES, (s + 1) * LANES)
+                out_ref[n, c, :, s, 0] = re[mine, lanes].reshape(-1, rows, LANES)
+                out_ref[n, c, :, s, 1] = im[mine, lanes].reshape(-1, rows, LANES)
+            copy = pltpu.make_async_copy(out_ref.at[n, c], out_hbm.at[:, segments], out_sems.at[n, c])
+            copy.start()
+            done.append(copy)
     for copy in done:
         copy.wait()
 
 
-def whiten(records, starts, rows):
+def whiten(records, starts, rows, chunks):
     count = records.shape[1]
     parts = 4
     splits = 2 if count % 2 == 0 else 1
+    per_chunk = F // chunks // rows
     tables = [jnp.asarray(t) for t in (hann_table(), *transform_tables())]
     return pl.pallas_call(
         whiten_kernel,
@@ -157,17 +161,17 @@
             pl.BlockSpec(memory_space=pltpu.SMEM),
             *[pl.BlockSpec(memory_space=pl.ANY) for _ in range(1 + len(tables))],
         ],
-        out_specs=pl.BlockSpec(memory_space=pl.ANY),
-        out_shape=jax.ShapeDtypeStruct((F // rows, count, 2, rows, LANES), jnp.float32),
+        out_specs=[pl.BlockSpec(memory_space=pl.ANY)] * chunks,
+        out_shape=[jax.ShapeDtypeStruct((per_chunk, count, 2, rows, LANES), jnp.float32)] * chunks,
         scratch_shapes=[
             pltpu.VMEM(records.shape, jnp.float32),
             *[pltpu.VMEM(t.shape, jnp.float32) for t in tables],
             pltpu.VMEM((4, count * LANES, 256), jnp.float32),
             pltpu.VMEM((F, F), jnp.bfloat16),
-            pltpu.VMEM((splits, F // rows, count // splits, 2, rows, LANES), jnp.float32),
+            pltpu.VMEM((splits, chunks, per_chunk, count // splits, 2, rows, LANES), jnp.float32),
             pltpu.SemaphoreType.DMA((len(tables),)),
             pltpu.SemaphoreType.DMA((parts,)),
-            pltpu.SemaphoreType.DMA((splits,)),
+            pltpu.SemaphoreType.DMA((splits, chunks)),
         ],
         compiler_params=pltpu.CompilerParams(vmem_limit_bytes=56 << 20),
     )(starts, records, *tables)
@@ -264,11 +268,20 @@
         scratch_shapes=[
             pltpu.VMEM((blocks, 2, terms * 2 * rows, LANES), jnp.bfloat16),
         ],
-        compiler_params=pltpu.CompilerParams(vmem_limit_bytes=32 << 20),
+        compiler_params=pltpu.CompilerParams(vmem_limit_bytes=10 << 20),
+        cost_estimate=pl.CostEstimate(
+            flops=8 * (2 * reach + 1) * LANES * pairs * LANES * spectra.size // LANES,
+            bytes_accessed=8 * spectra.size,
+            transcendentals=0,
+        ),
     )(index, spectra)
 
 
-def lag_kernel(cross_ref, turn_re_ref, turn_im_ref, even_ref, even_low_ref, odd_ref, odd_low_ref, out_hbm, out_ref, sems):
+def lag_kernel(cross_ref, turn_re_ref, turn_im_ref, even_ref, even_low_ref, odd_ref, odd_low_ref, *rest):
+    earlier_ref = rest[0] if len(rest) == 4 else None
+    last = len(rest) > 1
+    out_ref = rest[-2] if last else rest[0]
+    bins = cross_ref.shape[0] * cross_ref.shape[2]
     turn_re, turn_im = turn_re_ref[...], turn_im_ref[...]
     half = LAGS // 2
     mirror = LANES - 1 - lax.broadcasted_iota(jnp.int32, (LANES, LANES), 1)
@@ -281,60 +294,75 @@
     done = []
     for i in range(out_ref.shape[0]):
         lanes = slice(i * LANES, (i + 1) * LANES)
-        re = cross_ref[:, 0, :, lanes].reshape(F, LANES)
-        im = cross_ref[:, 1, :, lanes].reshape(F, LANES)
+        re = cross_ref[:, 0, :, lanes].reshape(bins, LANES)
+        im = cross_ref[:, 1, :, lanes].reshape(bins, LANES)
         re, im = re * turn_re + im * turn_im, im * turn_re - re * turn_im
         even = transform(re, even_ref, even_low_ref)
         odd = transform(im, odd_ref, odd_low_ref)
-        out_ref[i, :, half:] = even - odd
+        pieces = [(half, even - odd)]
         before = even + odd
         for first in range(0, half, LANES):
             turned = jnp.take_along_axis(before[:, first : first + LANES], mirror, axis=1)
-            out_ref[i, :, half - first - LANES : half - first] = turned
-        done.append(pltpu.make_async_copy(out_ref.at[i], out_hbm.at[i], sems.at[i]))
-        done[i].start()
+            pieces.append((half - first - LANES, turned))
+        for first, x in pieces:
+            at = slice(first, first + x.shape[1])
+            out_ref[i, :, at] = x if earlier_ref is None else x + earlier_ref[i, :, at]
+        if last:
+            done.append(pltpu.make_async_copy(out_ref.at[i], rest[-3].at[i], rest[-1].at[i]))
+            done[i].start()
     for copy in done:
         copy.wait()
 
 
-def lag_transform(cross, tables):
+def lag_transform(cross, tables, earlier, last):
     count = cross.shape[3] // LANES
+    given = [cross, *[jnp.asarray(t) for t in tables]]
+    if earlier is not None:
+        given.append(earlier)
+    shape = (count, LANES, LAGS)
     return pl.pallas_call(
         lag_kernel,
-        in_specs=[pl.BlockSpec(memory_space=pltpu.VMEM)] * (1 + len(tables)),
-        out_specs=pl.BlockSpec(memory_space=pl.ANY),
-        out_shape=jax.ShapeDtypeStruct((count, LANES, LAGS), jnp.float32),
-        scratch_shapes=[
-            pltpu.VMEM((count, LANES, LAGS), jnp.float32),
-            pltpu.SemaphoreType.DMA((count,)),
-        ],
-        compiler_params=pltpu.CompilerParams(vmem_limit_bytes=32 << 20),
-    )(cross, *[jnp.asarray(t) for t in tables])
+        in_specs=[pl.BlockSpec(memory_space=pltpu.VMEM)] * len(given),
+        out_specs=pl.BlockSpec(memory_space=pl.ANY if last else pltpu.VMEM),
+        out_shape=jax.ShapeDtypeStruct(shape, jnp.float32),
+        scratch_shapes=[pltpu.VMEM(shape, jnp.float32), pltpu.SemaphoreType.DMA((count,))] if last else [],
+        compiler_params=pltpu.CompilerParams(vmem_limit_bytes=10 << 20),
+        cost_estimate=pl.CostEstimate(
+            flops=6 * LAGS * cross.size, bytes_accessed=8 * cross.size, transcendentals=0
+        ),
+    )(*given)
 
 
 def local(records, starts, offsets):
     axes = ("blk", "inner")
     blocks, groups = lax.axis_size("blk"), lax.axis_size("inner")
     devices = blocks * groups
-    width = F // devices
     here, count = records.shape[:2]
     ids = jnp.arange(here, dtype=jnp.int32)[:, None] + REACH
     index = lax.all_gather((ids + offsets).T, "blk", axis=0)
+    chunks = 2 if F // devices % 16 == 0 else 1
+    width = F // devices // chunks
     rows = max(width, 8)
     split = rows // width
-    white = whiten(records, starts, rows)
-    white = white.reshape(-1, count // split, split, 2, split, width, LANES)
-    white = white.transpose(0, 4, 1, 3, 2, 5, 6).reshape(devices, -1, LANES)
-    spectra = lax.all_to_all(white, axes, 0, 0, tiled=True)
-    spectra = spectra.reshape(blocks, -1, 2, rows, LANES)
-    cross = pair_products(spectra, index, groups)
-    if split > 1:
-        cross = cross.reshape(blocks, groups, 2, split, width, -1).sum(3)
-    cross = lax.all_to_all(cross.reshape(devices, 2 * width, -1), axes, 0, 0, tiled=True)
-    cross = cross.reshape(devices, 2, width, -1)
-    if split > 1:
-        cross = cross.transpose(1, 0, 2, 3).reshape(1, 2, F, -1)
-    return lag_transform(cross, lag_tables(count * groups))
+    tables = lag_tables(count * groups)
+    lags = None
+    spectra = []
+    for white in whiten(records, starts, rows, chunks):
+        white = white.reshape(-1, count // split, split, 2, split, width, LANES)
+        white = white.transpose(0, 4, 1, 3, 2, 5, 6).reshape(devices, -1, LANES)
+        white = lax.all_to_all(white, axes, 0, 0, tiled=True)
+        spectra.append(white.reshape(blocks, -1, 2, rows, LANES))
+    for c in range(chunks):
+        cross = pair_products(spectra[c], index, groups)
+        if split > 1:
+            cross = cross.reshape(blocks, groups, 2, split, width, -1).sum(3)
+        cross = lax.all_to_all(cross.reshape(devices, 2 * width, -1), axes, 0, 0, tiled=True)
+        cross = cross.reshape(devices, 2, width, -1)
+        if split > 1:
+            cross = cross.transpose(1, 0, 2, 3).reshape(1, 2, F // chunks, -1)
+        mine = [t[c * F // chunks : (c + 1) * F // chunks] for t in tables]
+        lags = lag_transform(cross, mine, lags, c == chunks - 1)
+    return lags
 
 
 def solution(mesh):

time: 140 us -> 136 us (0.971)
  blocking collectives: 71.7 us -> 12.1 us
  waiting for transfers between devices: 28.6 us -> 61 us
  starting transfers between devices: 7.1 us -> 17.4 us
  local copies, waits for them, and re-layouts: 0.05 us -> 8.63 us
  Pallas kernels: 32.4 us -> 36.3 us
    all_to_all x1 -> x0, blocking collectives: 52.1 us -> none  [local(): lax.all_to_all(cross.reshape(devices, 2 * width, -1), axes, 0, 0, tiled=T...]
    all_to_all x1 -> x4, waiting for transfers between devices: 28.6 us -> 61 us  [the longest x2 32.1 us: local(): lax.all_to_all(cross.reshape(devices, 2 * width, -1), axes, 0, 0, tiled=T...]
    all_to_all x1 -> x4, starting transfers between devices: 7.1 us -> 17.4 us  [the longest x2 10.3 us: local(): white = lax.all_to_all(white, axes, 0, 0, tiled=True)]
    unnamed x14 -> x34, local copies, waits for them, and re-layouts: 0.05 us -> 8.63 us
    all_gather x1, blocking collectives: 19.6 us -> 12.1 us  [local(): index = lax.all_gather((ids + offsets).T, 'blk', axis=0)]
    pallas_call x1 -> x2, Pallas kernels: 19.3 us -> 23.3 us  [pair_products(): pl.pallas_call(functools.partial(pair_kernel, reach=reach, turned=turned)...]
    pallas_call x1 -> x2, Pallas kernels: 3.1 us -> 3.19 us  [lag_transform(): pl.pallas_call(lag_kernel, in_specs=[pl.BlockSpec(memory_space=pltpu.VMEM...]
  transfers between devices with their start and end apart: 1 -> 4, of which waited for: 1 -> 4; matrix products, arithmetic and copies ran while one was open for 0% -> 0% of each run, Pallas kernels for 0% -> 18%
where the time goes in v6:
time: 136 us
  waiting for transfers between devices  61 us (45%)
  Pallas kernels  36.3 us (27%)
  starting transfers between devices  17.4 us (13%)
  blocking collectives  12.1 us (9%)
  local copies, waits for them, and re-layouts  8.63 us (6%)
    all_to_all x2, waiting for transfers between devices, local(): lax.all_to_all(cross.reshape(devices, 2 * width, -1), axes, 0, 0, tiled=T...  32.1 us
    all_to_all x2, waiting for transfers between devices, local(): white = lax.all_to_all(white, axes, 0, 0, tiled=True)  28.9 us
    pallas_call x2, Pallas kernels, pair_products(): pl.pallas_call(functools.partial(pair_kernel, reach=reach, turned=turned)...  23.3 us
    all_gather x1, blocking collectives, local(): index = lax.all_gather((ids + offsets).T, 'blk', axis=0)  12.1 us
    all_to_all x2, starting transfers between devices, local(): white = lax.all_to_all(white, axes, 0, 0, tiled=True)  10.3 us
    pallas_call x1, Pallas kernels, whiten(): pl.pallas_call(whiten_kernel, in_specs=[pl.BlockSpec(memory_space=pltpu.S...  9.86 us
    unnamed x34, local copies, waits for them, and re-layouts  8.63 us
    all_to_all x2, starting transfers between devices, local(): lax.all_to_all(cross.reshape(devices, 2 * width, -1), axes, 0, 0, tiled=T...  7.1 us
  transfers between devices with their start and end apart: 4, of which 4 were waited for; matrix products, arithmetic and copies ran while one was open for 0% of the time, Pallas kernels for 18%

profile of v6, /device:TPU:1, one launch (start us, length us, event | category | flops | bytes accessed | tf_op | source)
XLA Modules:
  0.0 135.8 jit_solution(5171107854149422885)
XLA Ops:
  0.0 9.9 %shard_map.181 = (f32[32,4,2,8,128]{4,3,2,1,0:T(8,128)}, f32[32,4,2,8,128]{4,3,2,1,0:T(8,128)}) custom-call(s32[4]{0:T(128)} %starts_ref.1, f32[128,4,2048]{2,1,0:T(4,128)} %records_hbm.1, f32[8,1024]{1,0:T(8,128)} %constant.34.clone.hann_hbm, f32[256,256]{1,0:T(8,128)} %constant.35.clone.even0_hbm, f32[256,256]{1,0:T(8,128)} %constant.36.clone.even2_hbm, ...), custom_call_target="tpu_custom_call" | custom-call | tf_op jit(solution)/shard_map/pallas_call | solution.py:158
  9.9 7.1 %all-to-all-start.2 = ((f32[32,64,128]{2,1,0:T(8,128)}), f32[32,64,128]{2,1,0:T(8,128)S(1)}, u32[]{:S(2)}, u32[]{:S(2)}) async-start(f32[32,64,128]{2,1,0:T(8,128)} %bitcast.19), calls=%async_computation.2 | async-start | bytes 2097152 | tf_op jit(solution)/shard_map/all_to_all | solution.py:353
  17.0 26.3 %all-to-all-done.2 = f32[32,64,128]{2,1,0:T(8,128)S(1)} async-done(((f32[32,64,128]{2,1,0:T(8,128)}), f32[32,64,128]{2,1,0:T(8,128)S(1)}, u32[]{:S(2)}, u32[]{:S(2)}) %all-to-all-start.2) | async-done | bytes 1048608 | tf_op jit(solution)/shard_map/all_to_all | solution.py:353
  43.3 3.2 %all-to-all-start = ((f32[32,64,128]{2,1,0:T(8,128)}), f32[32,64,128]{2,1,0:T(8,128)S(1)}, u32[]{:S(2)}, u32[]{:S(2)}) async-start(f32[32,64,128]{2,1,0:T(8,128)} %bitcast.2), calls=%async_computation | async-start | bytes 2097152 | tf_op jit(solution)/shard_map/all_to_all | solution.py:353
  46.5 12.1 %all-gather = s32[128,128]{1,0:T(8,128)S(1)} all-gather(s32[16,128]{1,0:T(8,128)S(1)} %add_bitcast_fusion), channel_id=2, replica_groups=mesh['blk'=8,'inner'=4] {'blk'}, dimensions={0}, use_global_device_ids=true | all-gather | bytes 73728 | tf_op jit(solution)/shard_map/all_gather | solution.py:342
  58.6 11.6 %shard_map.183 = f32[8,4,2,8,512]{4,3,2,1,0:T(8,128)S(1)} custom-call(s32[8,16,128]{2,1,0:T(8,128)S(1)} %bitcast.17, f32[8,16,2,8,128]{4,3,2,1,0:T(8,128)S(1)} %bitcast.13), custom_call_target="tpu_custom_call" | custom-call | flops 21474836480 | bytes 2097152 | tf_op jit(solution)/shard_map/pallas_call | solution.py:263
  70.2 2.6 %all-to-all-done = f32[32,64,128]{2,1,0:T(8,128)S(1)} async-done(((f32[32,64,128]{2,1,0:T(8,128)}), f32[32,64,128]{2,1,0:T(8,128)S(1)}, u32[]{:S(2)}, u32[]{:S(2)}) %all-to-all-start) | async-done | bytes 1048608 | tf_op jit(solution)/shard_map/all_to_all | solution.py:353
  72.8 3.9 %all-to-all-start.3 = ((f32[32,16,512]{2,1,0:T(8,128)}), f32[32,16,512]{2,1,0:T(8,128)S(1)}, u32[]{:S(2)}, u32[]{:S(2)}) async-start(f32[32,16,512]{2,1,0:T(8,128)} %bitcast.16), calls=%async_computation.3 | async-start | bytes 2097152 | tf_op jit(solution)/shard_map/all_to_all | solution.py:359
  76.8 11.6 %shard_map.182 = f32[8,4,2,8,512]{4,3,2,1,0:T(8,128)S(1)} custom-call(s32[8,16,128]{2,1,0:T(8,128)S(1)} %bitcast.18, f32[8,16,2,8,128]{4,3,2,1,0:T(8,128)S(1)} %bitcast.14), custom_call_target="tpu_custom_call" | custom-call | flops 21474836480 | bytes 2097152 | tf_op jit(solution)/shard_map/pallas_call | solution.py:263
  88.4 1.0 copy-done.2
  89.4 13.7 %all-to-all-done.3 = f32[32,16,512]{2,1,0:T(8,128)S(1)} async-done(((f32[32,16,512]{2,1,0:T(8,128)}), f32[32,16,512]{2,1,0:T(8,128)S(1)}, u32[]{:S(2)}, u32[]{:S(2)}) %all-to-all-start.3) | async-done | bytes 1048608 | tf_op jit(solution)/shard_map/all_to_all | solution.py:359
  103.2 3.2 %all-to-all-start.1 = ((f32[32,16,512]{2,1,0:T(8,128)}), f32[32,16,512]{2,1,0:T(8,128)S(1)}, u32[]{:S(2)}, u32[]{:S(2)}) async-start(f32[32,16,512]{2,1,0:T(8,128)} %bitcast.15), calls=%async_computation.1 | async-start | bytes 2097152 | tf_op jit(solution)/shard_map/all_to_all | solution.py:359
  106.3 1.2 copy-done.1
  107.6 0.9 copy-done.10
  108.5 0.9 copy-done.11
  109.4 0.9 copy-done.12
  110.3 0.9 copy-done.13
  111.3 0.9 copy-done.14
  112.2 0.9 copy-done.15
  113.1 1.2 shard_map.184.rest_0_
  114.3 18.3 %all-to-all-done.1 = f32[32,16,512]{2,1,0:T(8,128)S(1)} async-done(((f32[32,16,512]{2,1,0:T(8,128)}), f32[32,16,512]{2,1,0:T(8,128)S(1)}, u32[]{:S(2)}, u32[]{:S(2)}) %all-to-all-start.1) | async-done | bytes 1048608 | tf_op jit(solution)/shard_map/all_to_all | solution.py:359
  132.7 0.0 copy-start.9
  132.7 0.9 copy-done.9
  133.6 2.0 %shard_map.185 = f32[4,128,768]{2,1,0:T(8,128)} custom-call(f32[32,2,8,512]{3,2,1,0:T(8,128)S(1)} %bitcast.11, f32[256,128]{1,0:T(8,128)S(1)} %copy-done.9, f32[256,128]{1,0:T(8,128)S(1)} %copy-done.8, bf16[256,384]{1,0:T(8,128)(2,1)S(1)} %copy-done.7, bf16[256,384]{1,0:T(8,128)(2,1)S(1)} %copy-done.6, bf16[256,384]{1,0:T(8,128)(2,1)S(1)} %copy-done.5, ...), custom_call_target="tpu_custom_call" | custom-call | flops 1207959552 | bytes 2097152 | tf_op jit(solution)/shard_map/pallas_call | solution.py:323
  (26 shorter events, 0.1 us)
Async XLA Ops:
  9.9 33.5 %all-to-all-start.2 = ((f32[32,64,128]{2,1,0:T(8,128)}), f32[32,64,128]{2,1,0:T(8,128)S(1)}, u32[]{:S(2)}, u32[]{:S(2)}) async-start(f32[32,64,128]{2,1,0:T(8,128)} %bitcast.19), calls=%async_computation.2 | async-start | bytes 2097152 | tf_op jit(solution)/shard_map/all_to_all | solution.py:353
  17.0 29.5 %copy-start.16 = (s32[128,16]{0,1:T(8,128)S(1)}, s32[128,16]{0,1:T(8,128)}, u32[]{:S(2)}) copy-start(s32[128,16]{0,1:T(8,128)} %param.21) | copy-start | bytes 24580
  43.3 29.5 %all-to-all-start = ((f32[32,64,128]{2,1,0:T(8,128)}), f32[32,64,128]{2,1,0:T(8,128)S(1)}, u32[]{:S(2)}, u32[]{:S(2)}) async-start(f32[32,64,128]{2,1,0:T(8,128)} %bitcast.2), calls=%async_computation | async-start | bytes 2097152 | tf_op jit(solution)/shard_map/all_to_all | solution.py:353
  70.2 2.6 %copy-start.3 = (f32[8,4,2,8,512]{4,3,2,1,0:T(8,128)}, f32[8,4,2,8,512]{4,3,2,1,0:T(8,128)S(1)}, u32[]{:S(2)}) copy-start(f32[8,4,2,8,512]{4,3,2,1,0:T(8,128)S(1)} %shard_map.183) | copy-start | bytes 3145732
  72.8 30.3 %all-to-all-start.3 = ((f32[32,16,512]{2,1,0:T(8,128)}), f32[32,16,512]{2,1,0:T(8,128)S(1)}, u32[]{:S(2)}, u32[]{:S(2)}) async-start(f32[32,16,512]{2,1,0:T(8,128)} %bitcast.16), calls=%async_computation.3 | async-start | bytes 2097152 | tf_op jit(solution)/shard_map/all_to_all | solution.py:359
  88.4 1.0 copy-start.2
  103.2 3.2 %copy-start = (f32[32,16,512]{2,1,0:T(8,128)}, f32[32,16,512]{2,1,0:T(8,128)S(1)}, u32[]{:S(2)}) copy-start(f32[32,16,512]{2,1,0:T(8,128)S(1)} %all-to-all-done.3) | copy-start | bytes 3145732
  103.2 29.5 %all-to-all-start.1 = ((f32[32,16,512]{2,1,0:T(8,128)}), f32[32,16,512]{2,1,0:T(8,128)S(1)}, u32[]{:S(2)}, u32[]{:S(2)}) async-start(f32[32,16,512]{2,1,0:T(8,128)} %bitcast.15), calls=%async_computation.1 | async-start | bytes 2097152 | tf_op jit(solution)/shard_map/all_to_all | solution.py:359
  106.3 1.2 copy-start.1
  107.6 0.9 copy-start.10
  108.5 0.9 copy-start.11
  109.4 0.9 copy-start.12
  110.3 0.9 copy-start.13
  111.3 0.9 copy-start.14
  112.2 0.9 copy-start.15
  113.1 19.6 %copy-start.4 = (bf16[256,384]{1,0:T(8,128)(2,1)S(1)}, bf16[256,384]{1,0:T(8,128)(2,1)}, u32[]{:S(2)}) copy-start(bf16[256,384]{1,0:T(8,128)(2,1)} %constant.49.clone.odd_low_ref) | copy-start | bytes 589828
  113.1 19.6 %copy-start.5 = (bf16[256,384]{1,0:T(8,128)(2,1)S(1)}, bf16[256,384]{1,0:T(8,128)(2,1)}, u32[]{:S(2)}) copy-start(bf16[256,384]{1,0:T(8,128)(2,1)} %constant.48.clone.odd_ref) | copy-start | bytes 589828
  113.1 19.6 %copy-start.6 = (bf16[256,384]{1,0:T(8,128)(2,1)S(1)}, bf16[256,384]{1,0:T(8,128)(2,1)}, u32[]{:S(2)}) copy-start(bf16[256,384]{1,0:T(8,128)(2,1)} %constant.47.clone.even_low_ref) | copy-start | bytes 589828
  113.1 19.6 %copy-start.7 = (bf16[256,384]{1,0:T(8,128)(2,1)S(1)}, bf16[256,384]{1,0:T(8,128)(2,1)}, u32[]{:S(2)}) copy-start(bf16[256,384]{1,0:T(8,128)(2,1)} %constant.46.clone.even_ref) | copy-start | bytes 589828
  113.1 19.6 %copy-start.8 = (f32[256,128]{1,0:T(8,128)S(1)}, f32[256,128]{1,0:T(8,128)}, u32[]{:S(2)}) copy-start(f32[256,128]{1,0:T(8,128)} %constant.45.clone.turn_im_ref) | copy-start | bytes 393220
  132.7 0.9 copy-start.9

commit v7 on v6

--- a/solution.py
+++ b/solution.py
@@ -36,14 +36,20 @@
 
 def lag_tables(segment_count):
     bins = bin_order()[:, None]
-    half = np.pi / SEG * bins * np.ones((1, LANES))
     angle = 2 * np.pi / SEG * bins * (np.arange(LAGS // 2)[None, :] + 0.5)
     factor = math.sqrt(segment_count / F) / segment_count
-    tables = [np.cos(half).astype(np.float32), np.sin(half).astype(np.float32)]
+    tables = []
     for table in (np.cos(angle) * factor, np.sin(angle) * factor):
         high = table.astype(jnp.bfloat16)
         tables += [high, (table - high.astype(np.float64)).astype(jnp.bfloat16)]
-    return tables
+    return np.stack(tables)
+
+
+def turn_table(devices, width, rows, chunks):
+    half = np.pi / SEG * bin_order().reshape(chunks, devices, 1, 1, width, 1)
+    half = np.broadcast_to(half, (chunks, devices, 1, rows // width, width, 1))
+    table = np.concatenate([np.cos(half), np.sin(half)], 2)
+    return jnp.asarray(table.reshape(chunks, devices, 2, rows, 1).astype(np.float32))
 
 
 def halves(x):
@@ -177,7 +183,7 @@
     )(starts, records, *tables)
 
 
-def pair_kernel(index_ref, spectra_ref, out_ref, wide_ref, *, reach, turned):
+def pair_kernel(index_ref, turn_ref, spectra_ref, out_ref, wide_ref, *, reach, turned):
     blocks, terms, _, rows, _ = spectra_ref.shape
 
     def build(i, carry):
@@ -188,13 +194,13 @@
     ids = lax.broadcasted_iota(jnp.int32, (LANES, LANES), 0)
 
     def one_block(block, carry):
-        pair_block(block, index_ref, spectra_ref, out_ref, wide_ref, ids, reach, turned)
+        pair_block(block, index_ref, turn_ref, spectra_ref, out_ref, wide_ref, ids, reach, turned)
         return carry
 
     lax.fori_loop(0, blocks, one_block, 0)
 
 
-def pair_block(block, index_ref, spectra_ref, out_ref, wide_ref, ids, reach, turned):
+def pair_block(block, index_ref, turn_ref, spectra_ref, out_ref, wide_ref, ids, reach, turned):
     blocks, terms, _, rows, _ = spectra_ref.shape
     pairs = index_ref.shape[1]
     groups = out_ref.shape[1]
@@ -203,9 +209,12 @@
     near = [lax.rem(block + (blocks - reach + j), blocks) for j in range(span)]
     left = jnp.concatenate([wide_ref[i, h] for i in near for h in range(2)], 1)
 
-    def put(k, h, rows_here, x):
+    def put(k, rows_here, re, im):
         z, q = k // share, k % share
-        out_ref[block, z, h, rows_here, q * LANES : (q + 1) * LANES] = x
+        turn_re, turn_im = turn_ref[0, rows_here], turn_ref[1, rows_here]
+        lanes = slice(q * LANES, (q + 1) * LANES)
+        out_ref[block, z, 0, rows_here, lanes] = re * turn_re + im * turn_im
+        out_ref[block, z, 1, rows_here, lanes] = im * turn_re - re * turn_im
 
     def by_product(ks):
         hots = []
@@ -224,8 +233,7 @@
                 own_re, own_im = spectra_ref[block, t, 0], spectra_ref[block, t, 1]
                 re = re + (own_re * partner_re + own_im * partner_im)
                 im = im + (own_im * partner_re - own_re * partner_im)
-            put(k, 0, slice(0, rows), re)
-            put(k, 1, slice(0, rows), im)
+            put(k, slice(0, rows), re, im)
 
     def by_gather(k, first):
         row = jnp.broadcast_to(index_ref[block, k : k + 1, :], (8, LANES))
@@ -244,8 +252,7 @@
             own_im = spectra_ref[block, t, 1, rows_here]
             re = re + (own_re * partner[0] + own_im * partner[1])
             im = im + (own_im * partner[0] - own_re * partner[1])
-        put(k, 0, rows_here, re)
-        put(k, 1, rows_here, im)
+        put(k, rows_here, re, im)
 
     chunks = [range(k, min(k + 2, pairs - turned)) for k in range(0, pairs - turned, 2)]
     gathers = [(k, first) for k in range(pairs - turned, pairs) for first in range(0, rows, 8)]
@@ -255,14 +262,14 @@
             by_gather(k, first)
 
 
-def pair_products(spectra, index, groups, turned=6):
+def pair_products(spectra, index, turn, groups, turned=6):
     blocks, terms, _, rows, _ = spectra.shape
     pairs = index.shape[1]
     reach = -(-REACH // LANES)
     shape = (groups, 2, rows, pairs // groups * LANES)
     return pl.pallas_call(
         functools.partial(pair_kernel, reach=reach, turned=turned),
-        in_specs=[pl.BlockSpec(memory_space=pltpu.VMEM)] * 2,
+        in_specs=[pl.BlockSpec(memory_space=pltpu.VMEM)] * 3,
         out_specs=pl.BlockSpec(memory_space=pltpu.VMEM),
         out_shape=jax.ShapeDtypeStruct((blocks, *shape), jnp.float32),
         scratch_shapes=[
@@ -274,31 +281,29 @@
             bytes_accessed=8 * spectra.size,
             transcendentals=0,
         ),
-    )(index, spectra)
-
-
-def lag_kernel(cross_ref, turn_re_ref, turn_im_ref, even_ref, even_low_ref, odd_ref, odd_low_ref, *rest):
+    )(index, turn, spectra)
+
+
+def lag_kernel(cross_ref, tables_ref, *rest):
     earlier_ref = rest[0] if len(rest) == 4 else None
     last = len(rest) > 1
     out_ref = rest[-2] if last else rest[0]
     bins = cross_ref.shape[0] * cross_ref.shape[2]
-    turn_re, turn_im = turn_re_ref[...], turn_im_ref[...]
     half = LAGS // 2
     mirror = LANES - 1 - lax.broadcasted_iota(jnp.int32, (LANES, LANES), 1)
 
-    def transform(x, high_ref, low_ref):
+    def transform(x, first):
         high, low = halves(x)
-        total = dot_tn(high, low_ref[...]) + dot_tn(low, high_ref[...])
-        return total + dot_tn(high, high_ref[...])
+        total = dot_tn(high, tables_ref[first + 1]) + dot_tn(low, tables_ref[first])
+        return total + dot_tn(high, tables_ref[first])
 
     done = []
     for i in range(out_ref.shape[0]):
         lanes = slice(i * LANES, (i + 1) * LANES)
         re = cross_ref[:, 0, :, lanes].reshape(bins, LANES)
         im = cross_ref[:, 1, :, lanes].reshape(bins, LANES)
-        re, im = re * turn_re + im * turn_im, im * turn_re - re * turn_im
-        even = transform(re, even_ref, even_low_ref)
-        odd = transform(im, odd_ref, odd_low_ref)
+        even = transform(re, 0)
+        odd = transform(im, 2)
         pieces = [(half, even - odd)]
         before = even + odd
         for first in range(0, half, LANES):
@@ -316,7 +321,7 @@
 
 def lag_transform(cross, tables, earlier, last):
     count = cross.shape[3] // LANES
-    given = [cross, *[jnp.asarray(t) for t in tables]]
+    given = [cross, jnp.asarray(tables)]
     if earlier is not None:
         given.append(earlier)
     shape = (count, LANES, LAGS)
@@ -345,6 +350,9 @@
     rows = max(width, 8)
     split = rows // width
     tables = lag_tables(count * groups)
+    device = lax.axis_index("blk") * groups + lax.axis_index("inner")
+    turns = lax.dynamic_index_in_dim(turn_table(devices, width, rows, chunks), device, 1, keepdims=False)
+    turns = jnp.broadcast_to(turns, (*turns.shape[:3], LANES))
     lags = None
     spectra = []
     for white in whiten(records, starts, rows, chunks):
@@ -353,14 +361,14 @@
         white = lax.all_to_all(white, axes, 0, 0, tiled=True)
         spectra.append(white.reshape(blocks, -1, 2, rows, LANES))
     for c in range(chunks):
-        cross = pair_products(spectra[c], index, groups)
+        cross = pair_products(spectra[c], index, turns[c], groups)
         if split > 1:
             cross = cross.reshape(blocks, groups, 2, split, width, -1).sum(3)
         cross = lax.all_to_all(cross.reshape(devices, 2 * width, -1), axes, 0, 0, tiled=True)
         cross = cross.reshape(devices, 2, width, -1)
         if split > 1:
             cross = cross.transpose(1, 0, 2, 3).reshape(1, 2, F // chunks, -1)
-        mine = [t[c * F // chunks : (c + 1) * F // chunks] for t in tables]
+        mine = tables[:, c * F // chunks : (c + 1) * F // chunks]
         lags = lag_transform(cross, mine, lags, c == chunks - 1)
     return lags
 

time: 136 us -> 135 us (level)
  waiting for transfers between devices: 61 us -> 65 us
  local copies, waits for them, and re-layouts: 8.63 us -> 5.15 us
    all_to_all x2, waiting for transfers between devices: 32.1 us -> 36.8 us  [local(): lax.all_to_all(cross.reshape(devices, 2 * width, -1), axes, 0, 0, tiled=T...]
    unnamed x34 -> x14, local copies, waits for them, and re-layouts: 8.63 us -> 4.31 us
  transfers between devices with their start and end apart: 4 -> 4, of which waited for: 4 -> 4; matrix products, arithmetic and copies ran while one was open for 0% -> 1% of each run, Pallas kernels for 18% -> 18%
where the time goes in v7:
time: 135 us; the launch traced here: 134 us
  waiting for transfers between devices  65 us (48%)
  Pallas kernels  35.5 us (26%)
  starting transfers between devices  17.1 us (13%)
  blocking collectives  11.4 us (8%)
  local copies, waits for them, and re-layouts  5.15 us (4%)
    all_to_all x2, waiting for transfers between devices, local(): lax.all_to_all(cross.reshape(devices, 2 * width, -1), axes, 0, 0, tiled=T...  36.8 us
    all_to_all x2, waiting for transfers between devices, local(): white = lax.all_to_all(white, axes, 0, 0, tiled=True)  28.2 us
    pallas_call x2, Pallas kernels, pair_products(): pl.pallas_call(functools.partial(pair_kernel, reach=reach, turned=turned)...  22.6 us
    all_gather x1, blocking collectives, local(): index = lax.all_gather((ids + offsets).T, 'blk', axis=0)  11.4 us
    all_to_all x2, starting transfers between devices, local(): white = lax.all_to_all(white, axes, 0, 0, tiled=True)  10.3 us
    pallas_call x1, Pallas kernels, whiten(): pl.pallas_call(whiten_kernel, in_specs=[pl.BlockSpec(memory_space=pltpu.S...  9.87 us
    all_to_all x2, starting transfers between devices, local(): lax.all_to_all(cross.reshape(devices, 2 * width, -1), axes, 0, 0, tiled=T...  6.88 us
    unnamed x14, local copies, waits for them, and re-layouts  4.31 us
  transfers between devices with their start and end apart: 4, of which 4 were waited for; matrix products, arithmetic and copies ran while one was open for 1% of the time, Pallas kernels for 18%

profile of v7, /device:TPU:1, one launch (start us, length us, event | category | flops | bytes accessed | tf_op | source)
XLA Modules:
  0.0 134.4 jit_solution(10873226083808839251)
XLA Ops:
  0.0 9.9 %shard_map.100 = (f32[32,4,2,8,128]{4,3,2,1,0:T(8,128)}, f32[32,4,2,8,128]{4,3,2,1,0:T(8,128)}) custom-call(s32[4]{0:T(128)} %starts_ref.1, f32[128,4,2048]{2,1,0:T(4,128)} %records_hbm.1, f32[8,1024]{1,0:T(8,128)} %constant.34.clone.hann_hbm, f32[256,256]{1,0:T(8,128)} %constant.35.clone.even0_hbm, f32[256,256]{1,0:T(8,128)} %constant.36.clone.even2_hbm, ...), custom_call_target="tpu_custom_call" | custom-call | tf_op jit(solution)/shard_map/pallas_call | solution.py:164
  9.9 0.0 copy-start.6
  9.9 7.1 %all-to-all-start.2 = ((f32[32,64,128]{2,1,0:T(8,128)}), f32[32,64,128]{2,1,0:T(8,128)S(1)}, u32[]{:S(2)}, u32[]{:S(2)}) async-start(f32[32,64,128]{2,1,0:T(8,128)} %bitcast.23), calls=%async_computation.2 | async-start | bytes 2097152 | tf_op jit(solution)/shard_map/all_to_all | solution.py:361
  17.0 26.3 %all-to-all-done.2 = f32[32,64,128]{2,1,0:T(8,128)S(1)} async-done(((f32[32,64,128]{2,1,0:T(8,128)}), f32[32,64,128]{2,1,0:T(8,128)S(1)}, u32[]{:S(2)}, u32[]{:S(2)}) %all-to-all-start.2) | async-done | bytes 1048608 | tf_op jit(solution)/shard_map/all_to_all | solution.py:361
  43.4 3.2 %all-to-all-start = ((f32[32,64,128]{2,1,0:T(8,128)}), f32[32,64,128]{2,1,0:T(8,128)S(1)}, u32[]{:S(2)}, u32[]{:S(2)}) async-start(f32[32,64,128]{2,1,0:T(8,128)} %bitcast.3), calls=%async_computation | async-start | bytes 2097152 | tf_op jit(solution)/shard_map/all_to_all | solution.py:361
  46.5 0.7 dynamic-slice_bitcast_fusion
  47.2 11.4 %all-gather = s32[128,128]{1,0:T(8,128)S(1)} all-gather(s32[16,128]{1,0:T(8,128)S(1)} %add_bitcast_fusion), channel_id=2, replica_groups=mesh['blk'=8,'inner'=4] {'blk'}, dimensions={0}, use_global_device_ids=true | all-gather | bytes 73728 | tf_op jit(solution)/shard_map/all_gather | solution.py:347
  58.6 0.1 broadcast_in_dim.15.turn_ref
  58.7 11.3 %shard_map.102 = f32[8,4,2,8,512]{4,3,2,1,0:T(8,128)S(1)} custom-call(s32[8,16,128]{2,1,0:T(8,128)S(1)} %bitcast.21, f32[2,8,128]{2,1,0:T(8,128)S(1)} %broadcast_in_dim.15.turn_ref, f32[8,16,2,8,128]{4,3,2,1,0:T(8,128)S(1)} %bitcast.16), custom_call_target="tpu_custom_call" | custom-call | flops 21474836480 | bytes 2097152 | tf_op jit(solution)/shard_map/pallas_call | solution.py:270
  70.0 1.0 copy-done.2
  71.0 1.9 %all-to-all-done = f32[32,64,128]{2,1,0:T(8,128)S(1)} async-done(((f32[32,64,128]{2,1,0:T(8,128)}), f32[32,64,128]{2,1,0:T(8,128)S(1)}, u32[]{:S(2)}, u32[]{:S(2)}) %all-to-all-start) | async-done | bytes 1048608 | tf_op jit(solution)/shard_map/all_to_all | solution.py:361
  72.9 3.7 %all-to-all-start.3 = ((f32[32,16,512]{2,1,0:T(8,128)}), f32[32,16,512]{2,1,0:T(8,128)S(1)}, u32[]{:S(2)}, u32[]{:S(2)}) async-start(f32[32,16,512]{2,1,0:T(8,128)} %bitcast.19), calls=%async_computation.3 | async-start | bytes 2097152 | tf_op jit(solution)/shard_map/all_to_all | solution.py:367
  76.6 0.1 broadcast_in_dim.13.turn_ref
  76.7 11.3 %shard_map.101 = f32[8,4,2,8,512]{4,3,2,1,0:T(8,128)S(1)} custom-call(s32[8,16,128]{2,1,0:T(8,128)S(1)} %bitcast.22, f32[2,8,128]{2,1,0:T(8,128)S(1)} %broadcast_in_dim.13.turn_ref, f32[8,16,2,8,128]{4,3,2,1,0:T(8,128)S(1)} %bitcast.17), custom_call_target="tpu_custom_call" | custom-call | flops 21474836480 | bytes 2097152 | tf_op jit(solution)/shard_map/pallas_call | solution.py:270
  88.0 0.0 copy-start.3
  88.0 1.0 copy-done.3
  89.0 14.0 %all-to-all-done.3 = f32[32,16,512]{2,1,0:T(8,128)S(1)} async-done(((f32[32,16,512]{2,1,0:T(8,128)}), f32[32,16,512]{2,1,0:T(8,128)S(1)}, u32[]{:S(2)}, u32[]{:S(2)}) %all-to-all-start.3) | async-done | bytes 1048608 | tf_op jit(solution)/shard_map/all_to_all | solution.py:367
  103.0 3.2 %all-to-all-start.1 = ((f32[32,16,512]{2,1,0:T(8,128)}), f32[32,16,512]{2,1,0:T(8,128)S(1)}, u32[]{:S(2)}, u32[]{:S(2)}) async-start(f32[32,16,512]{2,1,0:T(8,128)} %bitcast.20), calls=%async_computation.1 | async-start | bytes 2097152 | tf_op jit(solution)/shard_map/all_to_all | solution.py:367
  106.1 0.0 copy-done
  106.2 1.2 copy-done.1
  107.4 1.1 copy-done.5
  108.5 1.1 shard_map.103.rest_0_
  109.6 22.9 %all-to-all-done.1 = f32[32,16,512]{2,1,0:T(8,128)S(1)} async-done(((f32[32,16,512]{2,1,0:T(8,128)}), f32[32,16,512]{2,1,0:T(8,128)S(1)}, u32[]{:S(2)}, u32[]{:S(2)}) %all-to-all-start.1) | async-done | bytes 1048608 | tf_op jit(solution)/shard_map/all_to_all | solution.py:367
  132.5 1.9 %shard_map.104 = f32[4,128,768]{2,1,0:T(8,128)} custom-call(f32[32,2,8,512]{3,2,1,0:T(8,128)S(1)} %bitcast.15, bf16[4,256,384]{2,1,0:T(8,128)(2,1)S(1)} %copy-done.4, f32[4,128,768]{2,1,0:T(8,128)S(1)} %shard_map.103.rest_0_), custom_call_target="tpu_custom_call" | custom-call | flops 1207959552 | bytes 2097152 | tf_op jit(solution)/shard_map/pallas_call | solution.py:328
  (9 shorter events, 0.0 us)
Async XLA Ops:
  9.9 7.1 %copy-start.6 = (s32[128,16]{0,1:T(8,128)S(1)}, s32[128,16]{0,1:T(8,128)}, u32[]{:S(2)}) copy-start(s32[128,16]{0,1:T(8,128)} %param.12) | copy-start | bytes 24580
  9.9 33.5 %all-to-all-start.2 = ((f32[32,64,128]{2,1,0:T(8,128)}), f32[32,64,128]{2,1,0:T(8,128)S(1)}, u32[]{:S(2)}, u32[]{:S(2)}) async-start(f32[32,64,128]{2,1,0:T(8,128)} %bitcast.23), calls=%async_computation.2 | async-start | bytes 2097152 | tf_op jit(solution)/shard_map/all_to_all | solution.py:361
  43.4 29.5 %all-to-all-start = ((f32[32,64,128]{2,1,0:T(8,128)}), f32[32,64,128]{2,1,0:T(8,128)S(1)}, u32[]{:S(2)}, u32[]{:S(2)}) async-start(f32[32,64,128]{2,1,0:T(8,128)} %bitcast.3), calls=%async_computation | async-start | bytes 2097152 | tf_op jit(solution)/shard_map/all_to_all | solution.py:361
  70.0 1.0 copy-start.2
  72.9 30.1 %all-to-all-start.3 = ((f32[32,16,512]{2,1,0:T(8,128)}), f32[32,16,512]{2,1,0:T(8,128)S(1)}, u32[]{:S(2)}, u32[]{:S(2)}) async-start(f32[32,16,512]{2,1,0:T(8,128)} %bitcast.19), calls=%async_computation.3 | async-start | bytes 2097152 | tf_op jit(solution)/shard_map/all_to_all | solution.py:367
  88.0 1.0 copy-start.3
  103.0 3.2 %copy-start = (f32[32,16,512]{2,1,0:T(8,128)}, f32[32,16,512]{2,1,0:T(8,128)S(1)}, u32[]{:S(2)}) copy-start(f32[32,16,512]{2,1,0:T(8,128)S(1)} %all-to-all-done.3) | copy-start | bytes 3145732
  103.0 29.5 %all-to-all-start.1 = ((f32[32,16,512]{2,1,0:T(8,128)}), f32[32,16,512]{2,1,0:T(8,128)S(1)}, u32[]{:S(2)}, u32[]{:S(2)}) async-start(f32[32,16,512]{2,1,0:T(8,128)} %bitcast.20), calls=%async_computation.1 | async-start | bytes 2097152 | tf_op jit(solution)/shard_map/all_to_all | solution.py:367
  106.1 1.2 copy-start.1
  107.4 1.1 copy-start.5
  108.5 24.0 %copy-start.4 = (bf16[4,256,384]{2,1,0:T(8,128)(2,1)S(1)}, bf16[4,256,384]{2,1,0:T(8,128)(2,1)}, u32[]{:S(2)}) copy-start(bf16[4,256,384]{2,1,0:T(8,128)(2,1)} %constant.39.clone.tables_ref) | copy-start | bytes 2359300

commit v8 on v7

--- a/solution.py
+++ b/solution.py
@@ -158,7 +158,7 @@
 def whiten(records, starts, rows, chunks):
     count = records.shape[1]
     parts = 4
-    splits = 2 if count % 2 == 0 else 1
+    splits = 1
     per_chunk = F // chunks // rows
     tables = [jnp.asarray(t) for t in (hann_table(), *transform_tables())]
     return pl.pallas_call(

time: 135 us -> 133 us (0.985)
  Pallas kernels: 35.5 us -> 33.7 us
    pallas_call x1, Pallas kernels: 9.87 us -> 8.04 us  [whiten(): pl.pallas_call(whiten_kernel, in_specs=[pl.BlockSpec(memory_space=pltpu.S...]
where the time goes in v8:
time: 133 us
  waiting for transfers between devices  65 us (49%)
  Pallas kernels  33.7 us (25%)
  starting transfers between devices  17.1 us (13%)
  blocking collectives  11.4 us (9%)
  local copies, waits for them, and re-layouts  5.15 us (4%)
    all_to_all x2, waiting for transfers between devices, local(): lax.all_to_all(cross.reshape(devices, 2 * width, -1), axes, 0, 0, tiled=T...  36.9 us
    all_to_all x2, waiting for transfers between devices, local(): white = lax.all_to_all(white, axes, 0, 0, tiled=True)  28.2 us
    pallas_call x2, Pallas kernels, pair_products(): pl.pallas_call(functools.partial(pair_kernel, reach=reach, turned=turned)...  22.6 us
    all_gather x1, blocking collectives, local(): index = lax.all_gather((ids + offsets).T, 'blk', axis=0)  11.4 us
    all_to_all x2, starting transfers between devices, local(): white = lax.all_to_all(white, axes, 0, 0, tiled=True)  10.3 us
    pallas_call x1, Pallas kernels, whiten(): pl.pallas_call(whiten_kernel, in_specs=[pl.BlockSpec(memory_space=pltpu.S...  8.04 us
    all_to_all x2, starting transfers between devices, local(): lax.all_to_all(cross.reshape(devices, 2 * width, -1), axes, 0, 0, tiled=T...  6.88 us
    unnamed x14, local copies, waits for them, and re-layouts  4.31 us
  transfers between devices with their start and end apart: 4, of which 4 were waited for; matrix products, arithmetic and copies ran while one was open for 1% of the time, Pallas kernels for 18%

profile of v8, /device:TPU:1, one launch (start us, length us, event | category | flops | bytes accessed | tf_op | source)
XLA Modules:
  0.0 132.6 jit_solution(11339491391757317121)
XLA Ops:
  0.0 8.0 %shard_map.100 = (f32[32,4,2,8,128]{4,3,2,1,0:T(8,128)}, f32[32,4,2,8,128]{4,3,2,1,0:T(8,128)}) custom-call(s32[4]{0:T(128)} %starts_ref.1, f32[128,4,2048]{2,1,0:T(4,128)} %records_hbm.1, f32[8,1024]{1,0:T(8,128)} %constant.34.clone.hann_hbm, f32[256,256]{1,0:T(8,128)} %constant.35.clone.even0_hbm, f32[256,256]{1,0:T(8,128)} %constant.36.clone.even2_hbm, ...), custom_call_target="tpu_custom_call" | custom-call | tf_op jit(solution)/shard_map/pallas_call | solution.py:164
  8.0 0.0 copy-start.6
  8.1 7.1 %all-to-all-start.2 = ((f32[32,64,128]{2,1,0:T(8,128)}), f32[32,64,128]{2,1,0:T(8,128)S(1)}, u32[]{:S(2)}, u32[]{:S(2)}) async-start(f32[32,64,128]{2,1,0:T(8,128)} %bitcast.23), calls=%async_computation.2 | async-start | bytes 2097152 | tf_op jit(solution)/shard_map/all_to_all | solution.py:361
  15.2 0.0 copy-done.6
  15.2 26.3 %all-to-all-done.2 = f32[32,64,128]{2,1,0:T(8,128)S(1)} async-done(((f32[32,64,128]{2,1,0:T(8,128)}), f32[32,64,128]{2,1,0:T(8,128)S(1)}, u32[]{:S(2)}, u32[]{:S(2)}) %all-to-all-start.2) | async-done | bytes 1048608 | tf_op jit(solution)/shard_map/all_to_all | solution.py:361
  41.5 3.2 %all-to-all-start = ((f32[32,64,128]{2,1,0:T(8,128)}), f32[32,64,128]{2,1,0:T(8,128)S(1)}, u32[]{:S(2)}, u32[]{:S(2)}) async-start(f32[32,64,128]{2,1,0:T(8,128)} %bitcast.3), calls=%async_computation | async-start | bytes 2097152 | tf_op jit(solution)/shard_map/all_to_all | solution.py:361
  44.7 0.7 dynamic-slice_bitcast_fusion
  45.4 11.4 %all-gather = s32[128,128]{1,0:T(8,128)S(1)} all-gather(s32[16,128]{1,0:T(8,128)S(1)} %add_bitcast_fusion), channel_id=2, replica_groups=mesh['blk'=8,'inner'=4] {'blk'}, dimensions={0}, use_global_device_ids=true | all-gather | bytes 73728 | tf_op jit(solution)/shard_map/all_gather | solution.py:347
  56.8 0.1 broadcast_in_dim.15.turn_ref
  56.9 11.3 %shard_map.102 = f32[8,4,2,8,512]{4,3,2,1,0:T(8,128)S(1)} custom-call(s32[8,16,128]{2,1,0:T(8,128)S(1)} %bitcast.21, f32[2,8,128]{2,1,0:T(8,128)S(1)} %broadcast_in_dim.15.turn_ref, f32[8,16,2,8,128]{4,3,2,1,0:T(8,128)S(1)} %bitcast.16), custom_call_target="tpu_custom_call" | custom-call | flops 21474836480 | bytes 2097152 | tf_op jit(solution)/shard_map/pallas_call | solution.py:270
  68.2 1.0 copy-done.2
  69.2 1.8 %all-to-all-done = f32[32,64,128]{2,1,0:T(8,128)S(1)} async-done(((f32[32,64,128]{2,1,0:T(8,128)}), f32[32,64,128]{2,1,0:T(8,128)S(1)}, u32[]{:S(2)}, u32[]{:S(2)}) %all-to-all-start) | async-done | bytes 1048608 | tf_op jit(solution)/shard_map/all_to_all | solution.py:361
  71.0 3.7 %all-to-all-start.3 = ((f32[32,16,512]{2,1,0:T(8,128)}), f32[32,16,512]{2,1,0:T(8,128)S(1)}, u32[]{:S(2)}, u32[]{:S(2)}) async-start(f32[32,16,512]{2,1,0:T(8,128)} %bitcast.19), calls=%async_computation.3 | async-start | bytes 2097152 | tf_op jit(solution)/shard_map/all_to_all | solution.py:367
  74.8 0.1 broadcast_in_dim.13.turn_ref
  74.8 11.3 %shard_map.101 = f32[8,4,2,8,512]{4,3,2,1,0:T(8,128)S(1)} custom-call(s32[8,16,128]{2,1,0:T(8,128)S(1)} %bitcast.22, f32[2,8,128]{2,1,0:T(8,128)S(1)} %broadcast_in_dim.13.turn_ref, f32[8,16,2,8,128]{4,3,2,1,0:T(8,128)S(1)} %bitcast.17), custom_call_target="tpu_custom_call" | custom-call | flops 21474836480 | bytes 2097152 | tf_op jit(solution)/shard_map/pallas_call | solution.py:270
  86.2 0.0 copy-start.3
  86.2 1.0 copy-done.3
  87.1 14.0 %all-to-all-done.3 = f32[32,16,512]{2,1,0:T(8,128)S(1)} async-done(((f32[32,16,512]{2,1,0:T(8,128)}), f32[32,16,512]{2,1,0:T(8,128)S(1)}, u32[]{:S(2)}, u32[]{:S(2)}) %all-to-all-start.3) | async-done | bytes 1048608 | tf_op jit(solution)/shard_map/all_to_all | solution.py:367
  101.1 3.2 %all-to-all-start.1 = ((f32[32,16,512]{2,1,0:T(8,128)}), f32[32,16,512]{2,1,0:T(8,128)S(1)}, u32[]{:S(2)}, u32[]{:S(2)}) async-start(f32[32,16,512]{2,1,0:T(8,128)} %bitcast.20), calls=%async_computation.1 | async-start | bytes 2097152 | tf_op jit(solution)/shard_map/all_to_all | solution.py:367
  104.3 1.2 copy-done.1
  105.5 1.1 copy-done.5
  106.7 1.1 shard_map.103.rest_0_
  107.8 22.9 %all-to-all-done.1 = f32[32,16,512]{2,1,0:T(8,128)S(1)} async-done(((f32[32,16,512]{2,1,0:T(8,128)}), f32[32,16,512]{2,1,0:T(8,128)S(1)}, u32[]{:S(2)}, u32[]{:S(2)}) %all-to-all-start.1) | async-done | bytes 1048608 | tf_op jit(solution)/shard_map/all_to_all | solution.py:367
  130.7 1.9 %shard_map.104 = f32[4,128,768]{2,1,0:T(8,128)} custom-call(f32[32,2,8,512]{3,2,1,0:T(8,128)S(1)} %bitcast.15, bf16[4,256,384]{2,1,0:T(8,128)(2,1)S(1)} %copy-done.4, f32[4,128,768]{2,1,0:T(8,128)S(1)} %shard_map.103.rest_0_), custom_call_target="tpu_custom_call" | custom-call | flops 1207959552 | bytes 2097152 | tf_op jit(solution)/shard_map/pallas_call | solution.py:328
  (9 shorter events, 0.0 us)
Async XLA Ops:
  8.0 7.1 %copy-start.6 = (s32[128,16]{0,1:T(8,128)S(1)}, s32[128,16]{0,1:T(8,128)}, u32[]{:S(2)}) copy-start(s32[128,16]{0,1:T(8,128)} %param.12) | copy-start | bytes 24580
  8.1 33.5 %all-to-all-start.2 = ((f32[32,64,128]{2,1,0:T(8,128)}), f32[32,64,128]{2,1,0:T(8,128)S(1)}, u32[]{:S(2)}, u32[]{:S(2)}) async-start(f32[32,64,128]{2,1,0:T(8,128)} %bitcast.23), calls=%async_computation.2 | async-start | bytes 2097152 | tf_op jit(solution)/shard_map/all_to_all | solution.py:361
  41.5 29.5 %all-to-all-start = ((f32[32,64,128]{2,1,0:T(8,128)}), f32[32,64,128]{2,1,0:T(8,128)S(1)}, u32[]{:S(2)}, u32[]{:S(2)}) async-start(f32[32,64,128]{2,1,0:T(8,128)} %bitcast.3), calls=%async_computation | async-start | bytes 2097152 | tf_op jit(solution)/shard_map/all_to_all | solution.py:361
  68.2 1.0 copy-start.2
  71.0 30.1 %all-to-all-start.3 = ((f32[32,16,512]{2,1,0:T(8,128)}), f32[32,16,512]{2,1,0:T(8,128)S(1)}, u32[]{:S(2)}, u32[]{:S(2)}) async-start(f32[32,16,512]{2,1,0:T(8,128)} %bitcast.19), calls=%async_computation.3 | async-start | bytes 2097152 | tf_op jit(solution)/shard_map/all_to_all | solution.py:367
  86.2 1.0 copy-start.3
  101.1 3.2 %copy-start = (f32[32,16,512]{2,1,0:T(8,128)}, f32[32,16,512]{2,1,0:T(8,128)S(1)}, u32[]{:S(2)}) copy-start(f32[32,16,512]{2,1,0:T(8,128)S(1)} %all-to-all-done.3) | copy-start | bytes 3145732
  101.1 29.5 %all-to-all-start.1 = ((f32[32,16,512]{2,1,0:T(8,128)}), f32[32,16,512]{2,1,0:T(8,128)S(1)}, u32[]{:S(2)}, u32[]{:S(2)}) async-start(f32[32,16,512]{2,1,0:T(8,128)} %bitcast.20), calls=%async_computation.1 | async-start | bytes 2097152 | tf_op jit(solution)/shard_map/all_to_all | solution.py:367
  104.3 1.2 copy-start.1
  105.5 1.1 copy-start.5
  106.7 24.0 %copy-start.4 = (bf16[4,256,384]{2,1,0:T(8,128)(2,1)S(1)}, bf16[4,256,384]{2,1,0:T(8,128)(2,1)}, u32[]{:S(2)}) copy-start(bf16[4,256,384]{2,1,0:T(8,128)(2,1)} %constant.39.clone.tables_ref) | copy-start | bytes 2359300
